TPU v7x, 32 devices: a whole 2x2x4 slice. The times are simulated.
32 devices in a mesh: groups: 2 (over y), expert: 8 (over z, x), attn: 2 (over core).
Axes of the slice: x: 2, y: 2, z: 4, core: 2. Of those that a mesh axis runs over, the one named last changes fastest.
Arguments:
- tokens: bfloat16 [3, 512, 7168], P(None, ('groups', 'expert'), 'attn'), parts along dimension 1, may hold values from -6 to 6
- routes: int32 [3, 512, 8], P(None, ('groups', 'expert')), parts along dimension 1, may hold values from 0 to 255, all different within a row; in each aligned block of 32 rows (0 to 31, 32 to 63, ..., all dimensions but the last counted through in order) at most 2 rows name the same one
- route_weights: float32 [3, 512, 8], P(None, ('groups', 'expert')), parts along dimension 1, may hold values from 0.05 to 0.6
- gate_proj: bfloat16 [7168, 2048], P('attn', 'expert'), may hold values from -0.0625 to 0.0625
- up_proj: bfloat16 [7168, 2048], P('attn', 'expert'), may hold values from -0.0625 to 0.0625
- down_proj: bfloat16 [2048, 7168], P('expert', 'attn'), may hold values from -0.125 to 0.125
Outputs:
- mixed: bfloat16 [3, 512, 7168], P(None, ('groups', 'expert'), 'attn'), parts along dimension 1
There are 2 independent parts, one for each index of `groups`. A program takes and returns all parts, laid end to end along the dimension named above; an argument that names none is the same for every part. Nothing has to cross between parts.
Inputs may be any that keep to these rules, and one draw needn't show every extreme that they name: `routes`: the 8 numbers of a row differ. In each aligned block of 32 rows (the rows of one device in one step) no expert is named by more than 2 rows, a bound that some block reaches.
All inputs are finite; a program needn't handle non-finite values.
Results may differ from a plain program's by a relative error of at most 0.0057.
Values may be sent and summed in bfloat16 or wider, within the bound.
No kernel may reach another device: no remote copies, remote signals or barrier semaphores. Data moves between devices by JAX's collectives and lax.ppermute only.
A program may use at most 64 MiB of HBM per device.

v0:
```python
import jax
import jax.numpy as jnp
from jax import lax
from jax.sharding import PartitionSpec as P

EF = 2048
STEPS = 3
CAP = 2


def one_step(tokens, routes, route_weights, gate_proj, up_proj, down_proj):
    count, half = tokens.shape
    hidden_dev = gate_proj.shape[1]
    group = EF // hidden_dev
    experts_dev = lax.axis_size("expert")
    flight = experts_dev // group
    named = routes[:, :, None] == jnp.arange(flight, dtype=jnp.int32)[None, None, :]
    member = jnp.sum(named.astype(jnp.int32), axis=1)
    weights = jnp.sum(jnp.where(named, route_weights[:, :, None], 0.0), axis=1)
    before = jnp.cumsum(member, axis=0) - member
    picks = (member[None, :, :] == 1) & (
        before[None, :, :] == jnp.arange(CAP, dtype=jnp.int32)[:, None, None]
    )
    select = jnp.transpose(picks, (2, 0, 1)).astype(jnp.bfloat16)
    send_rows = jnp.einsum(
        "kcr,rd->kcd", select, tokens, preferred_element_type=jnp.float32
    ).astype(jnp.bfloat16)
    send_rows = jnp.repeat(send_rows, group, axis=0)
    got_rows = lax.all_to_all(send_rows, "expert", split_axis=0, concat_axis=0, tiled=True)
    slots = experts_dev * CAP
    restored = got_rows.reshape(slots, half)
    gate_part = jnp.dot(restored, gate_proj, preferred_element_type=jnp.float32)
    up_part = jnp.dot(restored, up_proj, preferred_element_type=jnp.float32)
    gate_full, up_full = lax.psum((gate_part, up_part), "attn")
    hidden = (jax.nn.silu(gate_full) * up_full).astype(jnp.bfloat16)
    partial_value = jnp.dot(hidden, down_proj, preferred_element_type=jnp.float32).astype(
        jnp.bfloat16
    )
    partial_value = partial_value.reshape(experts_dev, CAP, half)
    returned = lax.all_to_all(partial_value, "expert", split_axis=0, concat_axis=0, tiled=True)
    summed = jnp.sum(returned.astype(jnp.float32).reshape(flight, group, CAP, half), axis=1)
    scaled = select.astype(jnp.float32) * jnp.transpose(weights)[:, None, :]
    mixed = jnp.einsum("kcr,kcd->rd", scaled, summed, precision=lax.Precision.HIGHEST)
    return mixed.astype(jnp.bfloat16)


def local(tokens, routes, route_weights, gate_proj, up_proj, down_proj):
    outputs = [
        one_step(tokens[step], routes[step], route_weights[step], gate_proj, up_proj, down_proj)
        for step in range(STEPS)
    ]
    return jnp.stack(outputs, axis=0)


def solution(mesh):
    in_specs = (
        P(None, ("groups", "expert"), "attn"),
        P(None, ("groups", "expert"), None),
        P(None, ("groups", "expert"), None),
        P("attn", "expert"),
        P("attn", "expert"),
        P("expert", "attn"),
    )
    out_specs = P(None, ("groups", "expert"), "attn")
    return jax.shard_map(local, mesh=mesh, in_specs=in_specs, out_specs=out_specs, check_vma=False)
```

profile of v0, /device:TPU:0, one launch (start us, length us, event | category | flops | bytes accessed | tf_op | source)
XLA Modules:
  0.0 110.9 jit_solution(18044245703208196179)
XLA Ops:
  6.5 0.9 select_reduce_fusion.2
  7.5 0.1 copy.10
  7.6 0.1 reduce-window.21
  7.6 0.1 reduce.18
  7.8 1.1 convolution_convert_fusion.8
  8.8 0.7 reshape.598
  9.6 7.3 %all-to-all-start = ((bf16[8,2,3584]{2,1,0:T(2,128)(2,1)}), bf16[8,2,3584]{2,1,0:T(2,128)(2,1)S(1)}, u32[]{:S(2)}, u32[]{:S(2)}) async-start(bf16[8,2,3584]{2,1,0:T(2,128)(2,1)} %reshape.598), calls=%async_computation | async-start | bytes 229376 | tf_op jit(solution)/shard_map/all_to_all | solution.py:29
  16.8 0.1 copy.11
  16.9 0.1 reduce-window.22
  17.0 0.1 reduce.19
  17.1 0.1 copy.12
  17.2 0.1 reduce-window.23
  17.3 0.1 reduce.20
  17.4 1.1 convolution_convert_fusion.7
  18.5 1.1 convolution_convert_fusion.6
  19.6 4.5 %all-to-all-done = bf16[8,2,3584]{2,1,0:T(2,128)(2,1)S(1)} async-done(((bf16[8,2,3584]{2,1,0:T(2,128)(2,1)}), bf16[8,2,3584]{2,1,0:T(2,128)(2,1)S(1)}, u32[]{:S(2)}, u32[]{:S(2)}) %all-to-all-start) | async-done | bytes 114720 | tf_op jit(solution)/shard_map/all_to_all | solution.py:29
  24.0 0.7 reshape.608
  24.8 3.4 %all-to-all-start.4 = ((bf16[8,2,3584]{2,1,0:T(2,128)(2,1)}), bf16[8,2,3584]{2,1,0:T(2,128)(2,1)S(1)}, u32[]{:S(2)}, u32[]{:S(2)}) async-start(bf16[8,2,3584]{2,1,0:T(2,128)(2,1)} %reshape.608), calls=%async_computation.4 | async-start | bytes 229376 | tf_op jit(solution)/shard_map/all_to_all | solution.py:29
  28.2 2.6 %fusion.46 = f32[16,256]{1,0:T(8,128)} fusion(bf16[16,3584]{1,0:T(8,128)(2,1)S(1)} %reshape.599, bf16[3584,256]{1,0:T(8,128)(2,1)} %param.10), kind=kOutput, calls=%fused_computation.77 | convolution fusion | flops 29360128 | bytes 1966080 | tf_op jit(solution)/shard_map/dot_general | solution.py:33
  30.8 1.0 fusion.45
  31.7 3.6 %all-to-all-done.4 = bf16[8,2,3584]{2,1,0:T(2,128)(2,1)S(1)} async-done(((bf16[8,2,3584]{2,1,0:T(2,128)(2,1)}), bf16[8,2,3584]{2,1,0:T(2,128)(2,1)S(1)}, u32[]{:S(2)}, u32[]{:S(2)}) %all-to-all-start.4) | async-done | bytes 114720 | tf_op jit(solution)/shard_map/all_to_all | solution.py:29
  35.3 0.7 reshape.603
  36.0 3.4 %all-to-all-start.2 = ((bf16[8,2,3584]{2,1,0:T(2,128)(2,1)}), bf16[8,2,3584]{2,1,0:T(2,128)(2,1)S(1)}, u32[]{:S(2)}, u32[]{:S(2)}) async-start(bf16[8,2,3584]{2,1,0:T(2,128)(2,1)} %reshape.603), calls=%async_computation.2 | async-start | bytes 229376 | tf_op jit(solution)/shard_map/all_to_all | solution.py:29
  39.5 2.6 %fusion.50 = f32[16,256]{1,0:T(8,128)} fusion(bf16[16,3584]{1,0:T(8,128)(2,1)S(1)} %reshape.609, bf16[3584,256]{1,0:T(8,128)(2,1)} %param.10), kind=kOutput, calls=%fused_computation.81 | convolution fusion | flops 29360128 | bytes 1966080 | tf_op jit(solution)/shard_map/dot_general | solution.py:33
  42.1 0.9 fusion.49
  43.0 3.5 %all-to-all-done.2 = bf16[8,2,3584]{2,1,0:T(2,128)(2,1)S(1)} async-done(((bf16[8,2,3584]{2,1,0:T(2,128)(2,1)}), bf16[8,2,3584]{2,1,0:T(2,128)(2,1)S(1)}, u32[]{:S(2)}, u32[]{:S(2)}) %all-to-all-start.2) | async-done | bytes 114720 | tf_op jit(solution)/shard_map/all_to_all | solution.py:29
  46.6 2.6 %fusion.48 = f32[16,256]{1,0:T(8,128)} fusion(bf16[16,3584]{1,0:T(8,128)(2,1)S(1)} %reshape.604, bf16[3584,256]{1,0:T(8,128)(2,1)} %param.10), kind=kOutput, calls=%fused_computation.79 | convolution fusion | flops 29360128 | bytes 1966080 | tf_op jit(solution)/shard_map/dot_general | solution.py:33
  49.2 1.0 fusion.47
  50.2 16.4 %all-reduce.3.cloned.1.call-done = (f32[16,256]{1,0:T(8,128)}, f32[16,256]{1,0:T(8,128)}, f32[16,256]{1,0:T(8,128)}, f32[16,256]{1,0:T(8,128)}, f32[16,256]{1,0:T(8,128)}, /*index=5*/f32[16,256]{1,0:T(8,128)}) async-done(((f32[16,256]{1,0:T(8,128)}, f32[16,256]{1,0:T(8,128)}, f32[16,256]{1,0:T(8,128)}, f32[16,256]{1,0:T(8,128)}, f32[16,256]{1,0:T(8,128)}, /*index=5*/f32[16,256]{1,0:T(8,128)}), ...) | async-done | bytes 98320 | tf_op jit(solution)/shard_map/psum | solution.py:34
  66.6 1.1 convolution_convert_fusion.4
  67.7 0.7 reshape.605
  68.4 5.7 %all-to-all-start.3 = ((bf16[8,2,3584]{2,1,0:T(2,128)(2,1)}), bf16[8,2,3584]{2,1,0:T(2,128)(2,1)S(1)}, u32[]{:S(2)}, u32[]{:S(2)}) async-start(bf16[8,2,3584]{2,1,0:T(2,128)(2,1)} %reshape.605), calls=%async_computation.3 | async-start | bytes 229376 | tf_op jit(solution)/shard_map/all_to_all | solution.py:40
  74.2 0.3 convolution_convert_fusion.5
  74.5 0.7 reshape.600
  75.2 6.2 %all-to-all-done.3 = bf16[8,2,3584]{2,1,0:T(2,128)(2,1)S(1)} async-done(((bf16[8,2,3584]{2,1,0:T(2,128)(2,1)}), bf16[8,2,3584]{2,1,0:T(2,128)(2,1)S(1)}, u32[]{:S(2)}, u32[]{:S(2)}) %all-to-all-start.3) | async-done | bytes 114720 | tf_op jit(solution)/shard_map/all_to_all | solution.py:40
  81.4 3.4 %all-to-all-start.1 = ((bf16[8,2,3584]{2,1,0:T(2,128)(2,1)}), bf16[8,2,3584]{2,1,0:T(2,128)(2,1)S(1)}, u32[]{:S(2)}, u32[]{:S(2)}) async-start(bf16[8,2,3584]{2,1,0:T(2,128)(2,1)} %reshape.600), calls=%async_computation.1 | async-start | bytes 229376 | tf_op jit(solution)/shard_map/all_to_all | solution.py:40
  84.8 0.3 convolution_convert_fusion.3
  85.1 0.7 reshape.610
  85.8 0.1 convert_reduce_fusion.1
  85.9 6.0 %all-to-all-done.1 = bf16[8,2,3584]{2,1,0:T(2,128)(2,1)S(1)} async-done(((bf16[8,2,3584]{2,1,0:T(2,128)(2,1)}), bf16[8,2,3584]{2,1,0:T(2,128)(2,1)S(1)}, u32[]{:S(2)}, u32[]{:S(2)}) %all-to-all-start.1) | async-done | bytes 114720 | tf_op jit(solution)/shard_map/all_to_all | solution.py:40
  91.9 3.4 %all-to-all-start.5 = ((bf16[8,2,3584]{2,1,0:T(2,128)(2,1)}), bf16[8,2,3584]{2,1,0:T(2,128)(2,1)S(1)}, u32[]{:S(2)}, u32[]{:S(2)}) async-start(bf16[8,2,3584]{2,1,0:T(2,128)(2,1)} %reshape.610), calls=%async_computation.5 | async-start | bytes 229376 | tf_op jit(solution)/shard_map/all_to_all | solution.py:40
  95.3 0.1 convert_reduce_fusion.2
  95.4 0.6 fusion
  96.0 0.6 fusion.1
  96.6 5.8 %all-to-all-done.5 = bf16[8,2,3584]{2,1,0:T(2,128)(2,1)S(1)} async-done(((bf16[8,2,3584]{2,1,0:T(2,128)(2,1)}), bf16[8,2,3584]{2,1,0:T(2,128)(2,1)S(1)}, u32[]{:S(2)}, u32[]{:S(2)}) %all-to-all-start.5) | async-done | bytes 114720 | tf_op jit(solution)/shard_map/all_to_all | solution.py:40
  102.5 0.1 convert_reduce_fusion
  102.6 0.6 fusion.2
  103.2 0.9 pad_maximum_fusion
  (29 shorter events, 0.3 us)
Async XLA Ops:
  6.5 60.0 %copy-start = (bf16[256,3584]{1,0:T(8,128)(2,1)S(1)}, bf16[256,3584]{1,0:T(8,128)(2,1)}, u32[]{:S(2)}) copy-start(bf16[256,3584]{1,0:T(8,128)(2,1)} %param.11) | copy-start | bytes 5505028
  9.6 14.5 %all-to-all-start = ((bf16[8,2,3584]{2,1,0:T(2,128)(2,1)}), bf16[8,2,3584]{2,1,0:T(2,128)(2,1)S(1)}, u32[]{:S(2)}, u32[]{:S(2)}) async-start(bf16[8,2,3584]{2,1,0:T(2,128)(2,1)} %reshape.598), calls=%async_computation | async-start | bytes 229376 | tf_op jit(solution)/shard_map/all_to_all | solution.py:29
  24.8 10.5 %all-to-all-start.4 = ((bf16[8,2,3584]{2,1,0:T(2,128)(2,1)}), bf16[8,2,3584]{2,1,0:T(2,128)(2,1)S(1)}, u32[]{:S(2)}, u32[]{:S(2)}) async-start(bf16[8,2,3584]{2,1,0:T(2,128)(2,1)} %reshape.608), calls=%async_computation.4 | async-start | bytes 229376 | tf_op jit(solution)/shard_map/all_to_all | solution.py:29
  28.2 2.6 %copy-start.1 = (bf16[3584,256]{1,0:T(8,128)(2,1)S(1)}, bf16[3584,256]{1,0:T(8,128)(2,1)}, u32[]{:S(2)}) copy-start(bf16[3584,256]{1,0:T(8,128)(2,1)} %param.9) | copy-start | bytes 5505028
  36.0 10.5 %all-to-all-start.2 = ((bf16[8,2,3584]{2,1,0:T(2,128)(2,1)}), bf16[8,2,3584]{2,1,0:T(2,128)(2,1)S(1)}, u32[]{:S(2)}, u32[]{:S(2)}) async-start(bf16[8,2,3584]{2,1,0:T(2,128)(2,1)} %reshape.603), calls=%async_computation.2 | async-start | bytes 229376 | tf_op jit(solution)/shard_map/all_to_all | solution.py:29
  39.4 27.2 %all-reduce.3.cloned.1.call-start = ((), (), s32[]{:S(2)}) async-start(), calls=%async_computation.6 | async-start | bytes 196608 | tf_op jit(solution)/shard_map/psum | solution.py:34
  39.5 2.6 %copy-start.2 = (bf16[3584,256]{1,0:T(8,128)(2,1)S(1)}, bf16[3584,256]{1,0:T(8,128)(2,1)}, u32[]{:S(2)}) copy-start(bf16[3584,256]{1,0:T(8,128)(2,1)} %param.9) | copy-start | bytes 5505028
  46.6 2.6 %copy-start.3 = (bf16[3584,256]{1,0:T(8,128)(2,1)S(1)}, bf16[3584,256]{1,0:T(8,128)(2,1)}, u32[]{:S(2)}) copy-start(bf16[3584,256]{1,0:T(8,128)(2,1)} %param.9) | copy-start | bytes 5505028
  66.6 7.6 %copy-start.6 = (f32[16,256]{1,0:T(8,128)S(1)}, f32[16,256]{1,0:T(8,128)}, u32[]{:S(2)}) copy-start(f32[16,256]{1,0:T(8,128)} %get-tuple-element.12) | copy-start | bytes 49156
  66.6 7.6 %copy-start.7 = (f32[16,256]{1,0:T(8,128)S(1)}, f32[16,256]{1,0:T(8,128)}, u32[]{:S(2)}) copy-start(f32[16,256]{1,0:T(8,128)} %get-tuple-element.13) | copy-start | bytes 49156
  67.7 17.1 %copy-start.4 = (f32[16,256]{1,0:T(8,128)S(1)}, f32[16,256]{1,0:T(8,128)}, u32[]{:S(2)}) copy-start(f32[16,256]{1,0:T(8,128)} %get-tuple-element.8) | copy-start | bytes 49156
  67.7 17.1 %copy-start.5 = (f32[16,256]{1,0:T(8,128)S(1)}, f32[16,256]{1,0:T(8,128)}, u32[]{:S(2)}) copy-start(f32[16,256]{1,0:T(8,128)} %get-tuple-element.9) | copy-start | bytes 49156
  68.4 13.0 %all-to-all-start.3 = ((bf16[8,2,3584]{2,1,0:T(2,128)(2,1)}), bf16[8,2,3584]{2,1,0:T(2,128)(2,1)S(1)}, u32[]{:S(2)}, u32[]{:S(2)}) async-start(bf16[8,2,3584]{2,1,0:T(2,128)(2,1)} %reshape.605), calls=%async_computation.3 | async-start | bytes 229376 | tf_op jit(solution)/shard_map/all_to_all | solution.py:40
  81.4 10.5 %all-to-all-start.1 = ((bf16[8,2,3584]{2,1,0:T(2,128)(2,1)}), bf16[8,2,3584]{2,1,0:T(2,128)(2,1)S(1)}, u32[]{:S(2)}, u32[]{:S(2)}) async-start(bf16[8,2,3584]{2,1,0:T(2,128)(2,1)} %reshape.600), calls=%async_computation.1 | async-start | bytes 229376 | tf_op jit(solution)/shard_map/all_to_all | solution.py:40
  91.9 10.5 %all-to-all-start.5 = ((bf16[8,2,3584]{2,1,0:T(2,128)(2,1)}), bf16[8,2,3584]{2,1,0:T(2,128)(2,1)S(1)}, u32[]{:S(2)}, u32[]{:S(2)}) async-start(bf16[8,2,3584]{2,1,0:T(2,128)(2,1)} %reshape.610), calls=%async_computation.5 | async-start | bytes 229376 | tf_op jit(solution)/shard_map/all_to_all | solution.py:40
Sparse Core Ops, SparseCore 0:
  50.3 16.2 all-reduce.2
where the time goes:
time: 112 us; the launch traced here: 111 us
  waiting for transfers between devices  46 us (41%)
  starting transfers between devices  26.5 us (24%)
  matrix products  17.4 us (16%)
  between operations  13.6 us (12%)
  local copies, waits for them, and re-layouts  4.7 us (4%)
  other arithmetic  2.74 us (2%)
    all_to_all x3, waiting for transfers between devices, one_step(): lax.all_to_all(partial_value, 'expert', split_axis=0, concat_axis=0, tile...  18 us
    psum x1, waiting for transfers between devices, one_step(): gate_full, up_full = lax.psum((gate_part, up_part), 'attn')  16.4 us
    all_to_all x3, starting transfers between devices, one_step(): lax.all_to_all(send_rows, 'expert', split_axis=0, concat_axis=0, tiled=True)  14 us
    all_to_all x3, starting transfers between devices, one_step(): lax.all_to_all(partial_value, 'expert', split_axis=0, concat_axis=0, tile...  12.5 us
    all_to_all x3, waiting for transfers between devices, one_step(): lax.all_to_all(send_rows, 'expert', split_axis=0, concat_axis=0, tiled=True)  11.6 us
    dot_general x3, matrix products, one_step(): up_part = jnp.dot(restored, up_proj, preferred_element_type=jnp.float32)  7.76 us
    dot_general x3, matrix products, one_step(): jnp.einsum('kcr,rd->kcd', select, tokens, preferred_element_type=jnp.floa...  3.25 us
    dot_general x3, matrix products, one_step(): gate_part = jnp.dot(restored, gate_proj, preferred_element_type=jnp.float32)  2.85 us
  transfers between devices with their start and end apart: 7, of which 7 were waited for; matrix products, arithmetic and copies ran while one was open for 12% of the time, Pallas kernels for 0%

commit v1 on v0

v1 whole, which is shorter than its diff:
```python
import functools

import jax
import jax.numpy as jnp
from jax import lax
from jax.experimental import pallas as pl
from jax.experimental.pallas import tpu as pltpu
from jax.sharding import PartitionSpec as P

EF = 2048
STEPS = 3
CAP = 2
SLOTS = STEPS * CAP
PACK = 8
PIECES = 3
VMEM_BYTES = 48 * 1024 * 1024
BF16 = jnp.bfloat16
F32 = jnp.float32


def call(kernel, out_shape, *args, flops=0, bytes_accessed=0):
    return pl.pallas_call(
        kernel,
        out_shape=out_shape,
        in_specs=[pl.BlockSpec(memory_space=pltpu.VMEM)] * len(args),
        out_specs=jax.tree.map(lambda _: pl.BlockSpec(memory_space=pltpu.VMEM), out_shape),
        compiler_params=pltpu.CompilerParams(vmem_limit_bytes=VMEM_BYTES),
        cost_estimate=pl.CostEstimate(flops=flops, bytes_accessed=bytes_accessed, transcendentals=0),
    )(*args)


def dot(a, b):
    return jnp.dot(a, b, preferred_element_type=F32)


def slots_of(routes, expert_id):
    rows = routes.shape[0]
    per_step = rows // STEPS
    member = jnp.sum((routes == expert_id).astype(F32), axis=1, keepdims=True)
    at = lax.broadcasted_iota(jnp.int32, (rows, rows), 0)
    other = lax.broadcasted_iota(jnp.int32, (rows, rows), 1)
    earlier = (other < at) & (other // per_step == at // per_step)
    spread = jnp.broadcast_to(member, (rows, 128)).astype(BF16)
    before = dot(earlier.astype(BF16), spread)[:, :1].astype(jnp.int32)
    step = lax.broadcasted_iota(jnp.int32, (rows, 1), 0) // per_step
    return member > 0.5, step * CAP + before


def picks(member, slot, columns):
    rows = member.shape[0]
    lane = lax.broadcasted_iota(jnp.int32, (rows, columns), 1) % PACK
    main = member & (slot == lane) & (lane < SLOTS)
    rest = [
        member & (((lane == SLOTS) & (slot == t)) | ((lane == SLOTS + 1) & (slot == PIECES + t)))
        for t in range(PIECES)
    ]
    return main, rest


def select_kernel(flight, tokens_ref, routes_ref, out_ref):
    routes = routes_ref[...]
    piece = tokens_ref.shape[1] // (PIECES + 1)
    mains, rests = [], [[] for _ in range(PIECES)]
    for k in range(flight):
        member, slot = slots_of(routes, k)
        main, rest = picks(member, slot, PACK)
        mains.append(main.astype(F32))
        for t in range(PIECES):
            rests[t].append(rest[t].astype(F32))
    main = jnp.concatenate(mains, axis=1).T.astype(BF16)
    rest = jnp.concatenate([a for t in rests for a in t], axis=1).T.astype(BF16)
    last = dot(rest, tokens_ref[:, PIECES * piece :])
    count = flight * PACK
    for t in range(PIECES):
        cols = slice(t * piece, (t + 1) * piece)
        out_ref[:, cols] = (
            dot(main, tokens_ref[:, cols]) + last[t * count : (t + 1) * count]
        ).astype(BF16)


def gate_up_kernel(own_ref, one_ref, two_ref, three_ref, gate_ref, up_ref, out_ref):
    packed = own_ref.shape[1]
    piece = packed // PIECES
    hidden = gate_ref.shape[1]
    x = jnp.concatenate([r[...] for r in (own_ref, one_ref, two_ref, three_ref)], axis=0)
    rows = x.shape[0]
    tall = jnp.concatenate([x[:, t * piece : (t + 1) * piece] for t in range(PIECES)], axis=0)
    place = lax.broadcasted_iota(jnp.int32, (rows, hidden), 0) % PACK
    for h, ref in enumerate((gate_ref, up_ref)):
        total = dot(x, ref[:packed, :])
        last = dot(tall, ref[packed:, :])
        for t in range(PIECES):
            part = last[t * rows : (t + 1) * rows]
            low = pltpu.roll(part, rows - (SLOTS - t), 0)
            high = pltpu.roll(part, rows - (SLOTS + 1 - PIECES - t), 0)
            total = total + jnp.where(place == t, low, 0.0) + jnp.where(place == PIECES + t, high, 0.0)
        out_ref[:, h * hidden : (h + 1) * hidden] = total


def down_kernel(mine_ref, peer_ref, down_ref, *out_refs):
    rows = mine_ref.shape[0]
    depth = down_ref.shape[0]
    piece = down_ref.shape[1] // (PIECES + 1)
    total = mine_ref[...] + peer_ref[...]
    gate, up = total[:, :depth], total[:, depth:]
    hidden = (gate / (1.0 + jnp.exp(-gate)) * up).astype(BF16).astype(F32)
    place = lax.broadcasted_iota(jnp.int32, (rows, depth), 0) % PACK
    main = jnp.where(place < SLOTS, hidden, 0.0).astype(BF16)
    tall = jnp.concatenate(
        [
            jnp.where(place == SLOTS, pltpu.roll(hidden, SLOTS - t, 0), 0.0)
            + jnp.where(place == SLOTS + 1, pltpu.roll(hidden, SLOTS + 1 - PIECES - t, 0), 0.0)
            for t in range(PIECES)
        ],
        axis=0,
    ).astype(BF16)
    last = dot(tall, down_ref[:, PIECES * piece :])
    count = rows // len(out_refs)
    for t in range(PIECES):
        cols = slice(t * piece, (t + 1) * piece)
        part = (dot(main, down_ref[:, cols]) + last[t * rows : (t + 1) * rows]).astype(BF16)
        for b, ref in enumerate(out_refs):
            ref[:, cols] = part[b * count : (b + 1) * count]


def mix_kernel(flight, kept_ref, came_ref, routes_ref, weights_ref, out_ref):
    rows = routes_ref.shape[0]
    packed = kept_ref.shape[1]
    piece = packed // PIECES
    routes, scale = routes_ref[...], weights_ref[...]
    value = kept_ref[...] + came_ref[...].astype(F32)
    upper = value.astype(BF16).astype(F32)
    lower = value - upper
    first, last = None, None
    for k in range(flight):
        member, slot = slots_of(routes, k)
        weight = jnp.sum(jnp.where(routes == k, scale, 0.0), axis=1, keepdims=True)
        main, rest = picks(member, slot, 2 * PACK)
        take = slice(k * PACK, (k + 1) * PACK)
        both = jnp.concatenate([upper[take], lower[take]], axis=0).astype(BF16)
        one = weight * dot(main.astype(BF16), both)
        two = dot(rest[0].astype(BF16), both[:, :piece])
        for t in range(1, PIECES):
            two = two + dot(rest[t].astype(BF16), both[:, t * piece : (t + 1) * piece])
        two = weight * two
        first = one if first is None else first + one
        last = two if last is None else last + two
    out_ref[:, :packed] = first.astype(BF16)
    out_ref[:, packed:] = last.astype(BF16)


def local(tokens, routes, route_weights, gate_proj, up_proj, down_proj):
    steps, per_step, half = tokens.shape
    hidden_dev = gate_proj.shape[1]
    group = EF // hidden_dev
    devices = lax.axis_size("expert")
    flight = devices // group
    rows = steps * per_step
    packed = half // (PIECES + 1) * PIECES
    shape = jax.ShapeDtypeStruct
    tokens = tokens.reshape(rows, half)
    routes = routes.reshape(rows, routes.shape[2])
    route_weights = route_weights.reshape(rows, route_weights.shape[2])

    def swap(x, mask):
        return lax.ppermute(x, "expert", [(i, i ^ mask) for i in range(devices)])

    def across(x):
        if flight == 1:
            return x
        places = [[p + group * b for b in range(flight)] for p in range(group)]
        return lax.all_to_all(x, "expert", 0, 0, axis_index_groups=places, tiled=True)

    count = flight * PACK
    sent = call(
        functools.partial(select_kernel, flight), shape((count, packed), BF16), tokens, routes
    )
    sent = across(sent)
    pair = jnp.concatenate([sent, swap(sent, 4)], axis=0)
    came = [swap(pair, mask) for mask in (1, 2, 3)]
    all_rows = 8 * count
    products = call(
        gate_up_kernel,
        shape((all_rows, 2 * hidden_dev), F32),
        pair,
        *came,
        gate_proj,
        up_proj,
    )
    other = lax.ppermute(products, "attn", [(0, 1), (1, 0)])
    parts = call(
        down_kernel, [shape((2 * count, packed), BF16)] * 4, products, other, down_proj
    )
    back = [swap(parts[mask], mask) for mask in (1, 2, 3)]
    summed = parts[0].astype(F32)
    for x in back:
        summed = summed + x.astype(F32)
    kept, away = summed[:count], summed[count:].astype(BF16)
    came_back = swap(away, 4)
    if flight > 1:
        kept = across((kept + came_back.astype(F32)).astype(BF16)).astype(F32)
        came_back = jnp.zeros_like(came_back)
    mixed = call(
        functools.partial(mix_kernel, flight),
        shape((rows, half), BF16),
        kept,
        came_back,
        routes,
        route_weights,
    )
    return mixed.reshape(steps, per_step, half)


def solution(mesh):
    in_specs = (
        P(None, ("groups", "expert"), "attn"),
        P(None, ("groups", "expert"), None),
        P(None, ("groups", "expert"), None),
        P("attn", "expert"),
        P("attn", "expert"),
        P("expert", "attn"),
    )
    out_specs = P(None, ("groups", "expert"), "attn")
    return jax.shard_map(local, mesh=mesh, in_specs=in_specs, out_specs=out_specs, check_vma=False)
```

time: 112 us -> 37.1 us (0.33)
  waiting for transfers between devices: 46 us -> 14.4 us
  matrix products: 17.4 us -> 0 us
  between operations: 13.6 us -> 0.07 us
  starting transfers between devices: 26.5 us -> 13.8 us
  Pallas kernels: 0 us -> 3.48 us
  other arithmetic: 2.74 us -> 0.05 us
    all_to_all x6 -> x0, waiting for transfers between devices: 29.6 us -> none  [the longest x3 18 us: one_step(): lax.all_to_all(partial_value, 'expert', split_axis=0, concat_axis=0, tile...]
    all_to_all x6 -> x0, starting transfers between devices: 26.5 us -> none  [the longest x3 14 us: one_step(): lax.all_to_all(send_rows, 'expert', split_axis=0, concat_axis=0, tiled=True)]
    dot_general x15 -> x0, matrix products: 17.4 us -> none  [the longest x3 7.76 us: one_step(): up_part = jnp.dot(restored, up_proj, preferred_element_type=jnp.float32)]
    psum x1 -> x0, waiting for transfers between devices: 16.4 us -> none  [one_step(): gate_full, up_full = lax.psum((gate_part, up_part), 'attn')]
    ppermute x0 -> x9, waiting for transfers between devices: none -> 14.4 us  [the longest x8 13.1 us: swap(): return lax.ppermute(x, 'expert', [(i, i ^ mask) for i in range(devices)])]
    ppermute x0 -> x9, starting transfers between devices: none -> 13.8 us  [the longest x8 13.7 us: swap(): return lax.ppermute(x, 'expert', [(i, i ^ mask) for i in range(devices)])]
    unnamed x16 -> x12, local copies, waits for them, and re-layouts: 0.04 us -> 4.97 us
    reshape x9 -> x0, local copies, waits for them, and re-layouts: 4.4 us -> none  [the longest x3 2.13 us: one_step(): partial_value = partial_value.reshape(experts_dev, CAP, half)]
  transfers between devices with their start and end apart: 7 -> 9, of which waited for: 7 -> 9; matrix products, arithmetic and copies ran while one was open for 12% -> 0% of each run, Pallas kernels for 0% -> 0%
where the time goes in v1:
time: 37.1 us; the launch traced here: 36.8 us
  waiting for transfers between devices  14.4 us (39%)
  starting transfers between devices  13.8 us (37%)
  local copies, waits for them, and re-layouts  4.98 us (13%)
  Pallas kernels  3.48 us (9%)
    ppermute x8, starting transfers between devices, swap(): return lax.ppermute(x, 'expert', [(i, i ^ mask) for i in range(devices)])  13.7 us
    ppermute x8, waiting for transfers between devices, swap(): return lax.ppermute(x, 'expert', [(i, i ^ mask) for i in range(devices)])  13.1 us
    unnamed x12, local copies, waits for them, and re-layouts  4.97 us
    pallas_call x4, Pallas kernels, call(): pl.pallas_call(kernel, out_shape=out_shape, in_specs=[pl.BlockSpec(memory...  3.48 us
    ppermute x1, waiting for transfers between devices, local(): other = lax.ppermute(products, 'attn', [(0, 1), (1, 0)])  1.33 us
  transfers between devices with their start and end apart: 9, of which 9 were waited for; matrix products, arithmetic and copies ran while one was open for 0% of the time, Pallas kernels for 0%

profile of v1, /device:TPU:0, one launch (start us, length us, event | category | flops | bytes accessed | tf_op | source)
XLA Modules:
  0.0 36.8 jit_solution(7326922584115654870)
XLA Ops:
  0.0 0.8 %copy.7 = s32[3,32,8]{2,1,0:T(8,128)S(1)} copy(s32[3,32,8]{1,2,0:T(8,128)} %param.7) | data formatting | bytes 6144 | tf_op args[1]
  0.8 0.0 copy-start.3
  0.8 1.1 %copy-done.3 = bf16[3,32,3584]{2,1,0:T(8,128)(2,1)S(1)} copy-done((bf16[3,32,3584]{2,1,0:T(8,128)(2,1)S(1)}, bf16[3,32,3584]{2,1,0:T(8,128)(2,1)}, u32[]{:S(2)}) %copy-start.3) | copy-done | bytes 688152
  1.9 0.7 %shard_map.64 = bf16[8,2688]{1,0:T(8,128)(2,1)S(1)} custom-call(bf16[96,3584]{1,0:T(8,128)(2,1)S(1)} %bitcast.4, s32[96,8]{1,0:T(8,128)S(1)} %bitcast.5), custom_call_target="tpu_custom_call" | custom-call | tf_op jit(solution)/shard_map/pallas_call | solution.py:22
  2.5 4.1 %collective-permute-start = (bf16[8,2688]{1,0:T(8,128)(2,1)S(1)}, bf16[8,2688]{1,0:T(8,128)(2,1)S(1)}, u32[]{:S(2)}, u32[]{:S(2)}) collective-permute-start(bf16[8,2688]{1,0:T(8,128)(2,1)S(1)} %shard_map.64), channel_id=1, source_target_pairs={{0,8},{2,10},{4,12},{6,14},{8,0},{10,2},{12,4},{14,6},{1,9},{3,11}... | collective-permute-start | bytes 129032 | tf_op jit(solution)/shard_map/ppermute | solution.py:166
  6.7 2.5 %collective-permute-done = bf16[8,2688]{1,0:T(8,128)(2,1)S(1)} collective-permute-done((bf16[8,2688]{1,0:T(8,128)(2,1)S(1)}, bf16[8,2688]{1,0:T(8,128)(2,1)S(1)}, u32[]{:S(2)}, u32[]{:S(2)}) %collective-permute-start) | collective-permute-done | bytes 43040 | tf_op jit(solution)/shard_map/ppermute | solution.py:166
  9.1 2.4 %collective-permute-start.3 = (bf16[16,2688]{1,0:T(8,128)(2,1)S(1)}, bf16[16,2688]{1,0:T(8,128)(2,1)S(1)}, u32[]{:S(2)}, u32[]{:S(2)}) collective-permute-start(bf16[16,2688]{1,0:T(8,128)(2,1)S(1)} %pad_maximum_fusion.own_ref), channel_id=1, source_target_pairs={{0,6},{2,4},{4,2},{6,0},{8,14},{10,12},{12,10},{14,8},{1,7},{3,5},... | collective-permute-start | bytes 258056 | tf_op jit(solution)/shard_map/ppermute | solution.py:166
  11.6 0.8 %collective-permute-start.2 = (bf16[16,2688]{1,0:T(8,128)(2,1)S(1)}, bf16[16,2688]{1,0:T(8,128)(2,1)S(1)}, u32[]{:S(2)}, u32[]{:S(2)}) collective-permute-start(bf16[16,2688]{1,0:T(8,128)(2,1)S(1)} %pad_maximum_fusion.own_ref), channel_id=1, source_target_pairs={{0,4},{2,6},{4,0},{6,2},{8,12},{10,14},{12,8},{14,10},{1,5},{3,7},... | collective-permute-start | bytes 258056 | tf_op jit(solution)/shard_map/ppermute | solution.py:166
  12.3 0.3 collective-permute-start.1
  12.7 1.9 %collective-permute-done.3.three_ref = bf16[16,2688]{1,0:T(8,128)(2,1)S(1)} collective-permute-done((bf16[16,2688]{1,0:T(8,128)(2,1)S(1)}, bf16[16,2688]{1,0:T(8,128)(2,1)S(1)}, u32[]{:S(2)}, u32[]{:S(2)}) %collective-permute-start.3) | collective-permute-done | bytes 86048 | tf_op jit(solution)/shard_map/ppermute | solution.py:166
  14.6 1.5 %collective-permute-done.2.two_ref = bf16[16,2688]{1,0:T(8,128)(2,1)S(1)} collective-permute-done((bf16[16,2688]{1,0:T(8,128)(2,1)S(1)}, bf16[16,2688]{1,0:T(8,128)(2,1)S(1)}, u32[]{:S(2)}, u32[]{:S(2)}) %collective-permute-start.2) | collective-permute-done | bytes 86048 | tf_op jit(solution)/shard_map/ppermute | solution.py:166
  16.0 0.8 %collective-permute-done.1.one_ref = bf16[16,2688]{1,0:T(8,128)(2,1)S(1)} collective-permute-done((bf16[16,2688]{1,0:T(8,128)(2,1)S(1)}, bf16[16,2688]{1,0:T(8,128)(2,1)S(1)}, u32[]{:S(2)}, u32[]{:S(2)}) %collective-permute-start.1) | collective-permute-done | bytes 86048 | tf_op jit(solution)/shard_map/ppermute | solution.py:166
  16.8 0.0 copy-start
  16.8 1.5 %copy-done = bf16[3584,256]{1,0:T(8,128)(2,1)S(1)} copy-done((bf16[3584,256]{1,0:T(8,128)(2,1)S(1)}, bf16[3584,256]{1,0:T(8,128)(2,1)}, u32[]{:S(2)}) %copy-start) | copy-done | bytes 1835032
  18.3 0.0 copy-start.1
  18.3 1.5 %copy-done.1 = bf16[3584,256]{1,0:T(8,128)(2,1)S(1)} copy-done((bf16[3584,256]{1,0:T(8,128)(2,1)S(1)}, bf16[3584,256]{1,0:T(8,128)(2,1)}, u32[]{:S(2)}) %copy-start.1) | copy-done | bytes 1835032
  19.8 0.0 copy-start.2
  19.8 0.8 %shard_map.65.mine_ref = f32[64,512]{1,0:T(8,128)S(1)} custom-call(bf16[16,2688]{1,0:T(8,128)(2,1)S(1)} %pad_maximum_fusion.own_ref, bf16[16,2688]{1,0:T(8,128)(2,1)S(1)} %collective-permute-done.1.one_ref, bf16[16,2688]{1,0:T(8,128)(2,1)S(1)} %collective-permute-done.2.two_ref, bf16[16,2688]{1,0:T(8,128)(2,1)S(1)} %collective-permute-done.3.three_ref, ...), custom_call_target="tpu_custom_call" | custom-call | tf_op jit(solution)/shard_map/pallas_call | solution.py:22
  20.6 0.0 copy-start.4
  20.7 0.1 collective-permute-start.4
  20.7 1.3 %collective-permute-done.4.peer_ref = f32[64,512]{1,0:T(8,128)S(1)} collective-permute-done((f32[64,512]{1,0:T(8,128)S(1)}, f32[64,512]{1,0:T(8,128)S(1)}, u32[]{:S(2)}, u32[]{:S(2)}) %collective-permute-start.4) | collective-permute-done | bytes 131104 | tf_op jit(solution)/shard_map/ppermute | solution.py:190
  22.1 0.0 copy-done.2
  22.1 0.5 %shard_map.66 = (bf16[16,2688]{1,0:T(8,128)(2,1)S(1)}, bf16[16,2688]{1,0:T(8,128)(2,1)S(1)}, bf16[16,2688]{1,0:T(8,128)(2,1)S(1)}, bf16[16,2688]{1,0:T(8,128)(2,1)S(1)}) custom-call(f32[64,512]{1,0:T(8,128)S(1)} %shard_map.65.mine_ref, f32[64,512]{1,0:T(8,128)S(1)} %collective-permute-done.4.peer_ref, bf16[256,3584]{1,0:T(8,128)(2,1)S(1)} %copy-done.2), custom_call_target="tpu_custom_call" | custom-call | tf_op jit(solution)/shard_map/pallas_call | solution.py:22
  22.6 0.4 %collective-permute-start.5 = (bf16[16,2688]{1,0:T(8,128)(2,1)S(1)}, bf16[16,2688]{1,0:T(8,128)(2,1)S(1)}, u32[]{:S(2)}, u32[]{:S(2)}) collective-permute-start(bf16[16,2688]{1,0:T(8,128)(2,1)S(1)} %get-tuple-element.10), channel_id=1, source_target_pairs={{0,2},{2,0},{4,6},{6,4},{8,10},{10,8},{12,14},{14,12},{1,3},{3,1},... | collective-permute-start | bytes 258056 | tf_op jit(solution)/shard_map/ppermute | solution.py:166
  23.0 1.4 %collective-permute-start.6 = (bf16[16,2688]{1,0:T(8,128)(2,1)S(1)}, bf16[16,2688]{1,0:T(8,128)(2,1)S(1)}, u32[]{:S(2)}, u32[]{:S(2)}) collective-permute-start(bf16[16,2688]{1,0:T(8,128)(2,1)S(1)} %get-tuple-element.11), channel_id=1, source_target_pairs={{0,4},{2,6},{4,0},{6,2},{8,12},{10,14},{12,8},{14,10},{1,5},{3,7},... | collective-permute-start | bytes 258056 | tf_op jit(solution)/shard_map/ppermute | solution.py:166
  24.4 1.7 %collective-permute-start.7 = (bf16[16,2688]{1,0:T(8,128)(2,1)S(1)}, bf16[16,2688]{1,0:T(8,128)(2,1)S(1)}, u32[]{:S(2)}, u32[]{:S(2)}) collective-permute-start(bf16[16,2688]{1,0:T(8,128)(2,1)S(1)} %get-tuple-element.12), channel_id=1, source_target_pairs={{0,6},{2,4},{4,2},{6,0},{8,14},{10,12},{12,10},{14,8},{1,7},{3,5},... | collective-permute-start | bytes 258056 | tf_op jit(solution)/shard_map/ppermute | solution.py:166
  26.1 1.1 %collective-permute-done.5 = bf16[16,2688]{1,0:T(8,128)(2,1)S(1)} collective-permute-done((bf16[16,2688]{1,0:T(8,128)(2,1)S(1)}, bf16[16,2688]{1,0:T(8,128)(2,1)S(1)}, u32[]{:S(2)}, u32[]{:S(2)}) %collective-permute-start.5) | collective-permute-done | bytes 86048 | tf_op jit(solution)/shard_map/ppermute | solution.py:166
  27.2 0.3 collective-permute-done.6
  27.5 2.8 %collective-permute-done.7 = bf16[16,2688]{1,0:T(8,128)(2,1)S(1)} collective-permute-done((bf16[16,2688]{1,0:T(8,128)(2,1)S(1)}, bf16[16,2688]{1,0:T(8,128)(2,1)S(1)}, u32[]{:S(2)}, u32[]{:S(2)}) %collective-permute-start.7) | collective-permute-done | bytes 86048 | tf_op jit(solution)/shard_map/ppermute | solution.py:166
  30.3 2.5 %collective-permute-start.8 = (bf16[8,2688]{1,0:T(8,128)(2,1)S(1)}, bf16[8,2688]{1,0:T(8,128)(2,1)S(1)}, u32[]{:S(2)}, u32[]{:S(2)}) collective-permute-start(bf16[8,2688]{1,0:T(8,128)(2,1)S(1)} %slice.12), channel_id=1, source_target_pairs={{0,8},{2,10},{4,12},{6,14},{8,0},{10,2},{12,4},{14,6},{1,9},{3,11}... | collective-permute-start | bytes 129032 | tf_op jit(solution)/shard_map/ppermute | solution.py:166
  32.8 0.0 copy-done.4
  32.9 0.1 copy.8
  32.9 2.4 %collective-permute-done.8.came_ref = bf16[8,2688]{1,0:T(8,128)(2,1)S(1)} collective-permute-done((bf16[8,2688]{1,0:T(8,128)(2,1)S(1)}, bf16[8,2688]{1,0:T(8,128)(2,1)S(1)}, u32[]{:S(2)}, u32[]{:S(2)}) %collective-permute-start.8) | collective-permute-done | bytes 43040 | tf_op jit(solution)/shard_map/ppermute | solution.py:166
  35.3 1.5 %shard_map.67 = bf16[96,3584]{1,0:T(8,128)(2,1)} custom-call(f32[8,2688]{1,0:T(8,128)S(1)} %slice.9.kept_ref, bf16[8,2688]{1,0:T(8,128)(2,1)S(1)} %collective-permute-done.8.came_ref, s32[96,8]{1,0:T(8,128)S(1)} %bitcast.6, f32[96,8]{1,0:T(8,128)S(1)} %bitcast.7), custom_call_target="tpu_custom_call" | custom-call | tf_op jit(solution)/shard_map/pallas_call | solution.py:22
  (4 shorter events, 0.1 us)
Async XLA Ops:
  0.8 1.1 %copy-start.3 = (bf16[3,32,3584]{2,1,0:T(8,128)(2,1)S(1)}, bf16[3,32,3584]{2,1,0:T(8,128)(2,1)}, u32[]{:S(2)}) copy-start(bf16[3,32,3584]{2,1,0:T(8,128)(2,1)} %param.6) | copy-start | bytes 2064388
  2.5 6.6 %collective-permute-start = (bf16[8,2688]{1,0:T(8,128)(2,1)S(1)}, bf16[8,2688]{1,0:T(8,128)(2,1)S(1)}, u32[]{:S(2)}, u32[]{:S(2)}) collective-permute-start(bf16[8,2688]{1,0:T(8,128)(2,1)S(1)} %shard_map.64), channel_id=1, source_target_pairs={{0,8},{2,10},{4,12},{6,14},{8,0},{10,2},{12,4},{14,6},{1,9},{3,11}... | collective-permute-start | bytes 129032 | tf_op jit(solution)/shard_map/ppermute | solution.py:166
  9.1 5.4 %collective-permute-start.3 = (bf16[16,2688]{1,0:T(8,128)(2,1)S(1)}, bf16[16,2688]{1,0:T(8,128)(2,1)S(1)}, u32[]{:S(2)}, u32[]{:S(2)}) collective-permute-start(bf16[16,2688]{1,0:T(8,128)(2,1)S(1)} %pad_maximum_fusion.own_ref), channel_id=1, source_target_pairs={{0,6},{2,4},{4,2},{6,0},{8,14},{10,12},{12,10},{14,8},{1,7},{3,5},... | collective-permute-start | bytes 258056 | tf_op jit(solution)/shard_map/ppermute | solution.py:166
  11.6 4.5 %collective-permute-start.2 = (bf16[16,2688]{1,0:T(8,128)(2,1)S(1)}, bf16[16,2688]{1,0:T(8,128)(2,1)S(1)}, u32[]{:S(2)}, u32[]{:S(2)}) collective-permute-start(bf16[16,2688]{1,0:T(8,128)(2,1)S(1)} %pad_maximum_fusion.own_ref), channel_id=1, source_target_pairs={{0,4},{2,6},{4,0},{6,2},{8,12},{10,14},{12,8},{14,10},{1,5},{3,7},... | collective-permute-start | bytes 258056 | tf_op jit(solution)/shard_map/ppermute | solution.py:166
  12.3 4.5 %collective-permute-start.1 = (bf16[16,2688]{1,0:T(8,128)(2,1)S(1)}, bf16[16,2688]{1,0:T(8,128)(2,1)S(1)}, u32[]{:S(2)}, u32[]{:S(2)}) collective-permute-start(bf16[16,2688]{1,0:T(8,128)(2,1)S(1)} %pad_maximum_fusion.own_ref), channel_id=1, source_target_pairs={{0,2},{2,0},{4,6},{6,4},{8,10},{10,8},{12,14},{14,12},{1,3},{3,1},... | collective-permute-start | bytes 258056 | tf_op jit(solution)/shard_map/ppermute | solution.py:166
  16.8 1.5 %copy-start = (bf16[3584,256]{1,0:T(8,128)(2,1)S(1)}, bf16[3584,256]{1,0:T(8,128)(2,1)}, u32[]{:S(2)}) copy-start(bf16[3584,256]{1,0:T(8,128)(2,1)} %gate_ref.1) | copy-start | bytes 5505028
  18.3 1.5 %copy-start.1 = (bf16[3584,256]{1,0:T(8,128)(2,1)S(1)}, bf16[3584,256]{1,0:T(8,128)(2,1)}, u32[]{:S(2)}) copy-start(bf16[3584,256]{1,0:T(8,128)(2,1)} %up_ref.1) | copy-start | bytes 5505028
  19.8 2.2 %copy-start.2 = (bf16[256,3584]{1,0:T(8,128)(2,1)S(1)}, bf16[256,3584]{1,0:T(8,128)(2,1)}, u32[]{:S(2)}) copy-start(bf16[256,3584]{1,0:T(8,128)(2,1)} %down_ref.1) | copy-start | bytes 5505028
  20.6 12.2 %copy-start.4 = (f32[3,32,8]{1,2,0:T(8,128)S(1)}, f32[3,32,8]{1,2,0:T(8,128)}, u32[]{:S(2)}) copy-start(f32[3,32,8]{1,2,0:T(8,128)} %param.8) | copy-start | bytes 9220
  20.7 1.4 %collective-permute-start.4 = (f32[64,512]{1,0:T(8,128)S(1)}, f32[64,512]{1,0:T(8,128)S(1)}, u32[]{:S(2)}, u32[]{:S(2)}) collective-permute-start(f32[64,512]{1,0:T(8,128)S(1)} %shard_map.65.mine_ref), channel_id=1, source_target_pairs={{0,1},{1,0},{2,3},{3,2},{4,5},{5,4},{6,7},{7,6},{8,9},{9,8},{10,11... | collective-permute-start | bytes 393224 | tf_op jit(solution)/shard_map/ppermute | solution.py:190
  22.6 4.7 %collective-permute-start.5 = (bf16[16,2688]{1,0:T(8,128)(2,1)S(1)}, bf16[16,2688]{1,0:T(8,128)(2,1)S(1)}, u32[]{:S(2)}, u32[]{:S(2)}) collective-permute-start(bf16[16,2688]{1,0:T(8,128)(2,1)S(1)} %get-tuple-element.10), channel_id=1, source_target_pairs={{0,2},{2,0},{4,6},{6,4},{8,10},{10,8},{12,14},{14,12},{1,3},{3,1},... | collective-permute-start | bytes 258056 | tf_op jit(solution)/shard_map/ppermute | solution.py:166
  23.0 4.5 %collective-permute-start.6 = (bf16[16,2688]{1,0:T(8,128)(2,1)S(1)}, bf16[16,2688]{1,0:T(8,128)(2,1)S(1)}, u32[]{:S(2)}, u32[]{:S(2)}) collective-permute-start(bf16[16,2688]{1,0:T(8,128)(2,1)S(1)} %get-tuple-element.11), channel_id=1, source_target_pairs={{0,4},{2,6},{4,0},{6,2},{8,12},{10,14},{12,8},{14,10},{1,5},{3,7},... | collective-permute-start | bytes 258056 | tf_op jit(solution)/shard_map/ppermute | solution.py:166
  24.4 5.8 %collective-permute-start.7 = (bf16[16,2688]{1,0:T(8,128)(2,1)S(1)}, bf16[16,2688]{1,0:T(8,128)(2,1)S(1)}, u32[]{:S(2)}, u32[]{:S(2)}) collective-permute-start(bf16[16,2688]{1,0:T(8,128)(2,1)S(1)} %get-tuple-element.12), channel_id=1, source_target_pairs={{0,6},{2,4},{4,2},{6,0},{8,14},{10,12},{12,10},{14,8},{1,7},{3,5},... | collective-permute-start | bytes 258056 | tf_op jit(solution)/shard_map/ppermute | solution.py:166
  30.3 5.0 %collective-permute-start.8 = (bf16[8,2688]{1,0:T(8,128)(2,1)S(1)}, bf16[8,2688]{1,0:T(8,128)(2,1)S(1)}, u32[]{:S(2)}, u32[]{:S(2)}) collective-permute-start(bf16[8,2688]{1,0:T(8,128)(2,1)S(1)} %slice.12), channel_id=1, source_target_pairs={{0,8},{2,10},{4,12},{6,14},{8,0},{10,2},{12,4},{14,6},{1,9},{3,11}... | collective-permute-start | bytes 129032 | tf_op jit(solution)/shard_map/ppermute | solution.py:166

commit v2 on v1

v2 whole, which is shorter than its diff:
```python
import functools

import jax
import jax.numpy as jnp
from jax import lax
from jax.experimental import pallas as pl
from jax.experimental.pallas import tpu as pltpu
from jax.sharding import PartitionSpec as P

EF = 2048
STEPS = 3
CAP = 2
SLOTS = STEPS * CAP
PACK = 8
PIECES = 3
QUAD = (3, 2, 1)
LOADS = 4
MIB = 1024 * 1024
VMEM_BYTES = 32 * MIB
BF16 = jnp.bfloat16
F32 = jnp.float32


def call(kernel, out_shape, *args, scratch=(), here=(), out_here=False, cost=0, room=VMEM_BYTES):
    vmem, hbm = pl.BlockSpec(memory_space=pltpu.VMEM), pl.BlockSpec(memory_space=pltpu.HBM)
    return pl.pallas_call(
        kernel,
        out_shape=out_shape,
        in_specs=[hbm if i in here else vmem for i in range(len(args))],
        out_specs=jax.tree.map(lambda _: hbm if out_here else vmem, out_shape),
        scratch_shapes=scratch,
        compiler_params=pltpu.CompilerParams(vmem_limit_bytes=room),
        cost_estimate=pl.CostEstimate(flops=0, bytes_accessed=cost, transcendentals=0),
    )(*args)


def dot(a, b):
    return jnp.dot(a, b, preferred_element_type=F32)


def slots_of(routes, expert_id, step):
    choices, rows = routes.shape
    member = jnp.max((routes == expert_id).astype(F32), axis=0, keepdims=True)
    other = lax.broadcasted_iota(jnp.int32, (rows, rows), 0)
    at = lax.broadcasted_iota(jnp.int32, (rows, rows), 1)
    spread = jnp.broadcast_to(member, (choices, rows)).astype(BF16)
    before = dot(spread, (other < at).astype(BF16))[:1].astype(jnp.int32)
    return member > 0.5, step * CAP + before


def pick_kernel(flight, routes_ref, out_ref):
    steps, _, rows = routes_ref.shape
    place = lax.broadcasted_iota(jnp.int32, (PACK, rows), 0)
    for s in range(steps):
        routes = routes_ref[s]
        picked = [[] for _ in range(PIECES + 1)]
        for k in range(flight):
            member, slot = slots_of(routes, k, s)
            picked[0].append((member & (slot == place)).astype(F32))
            for t in range(PIECES):
                of_six = (place == SLOTS) & (slot == t)
                of_seven = (place == SLOTS + 1) & (slot == PIECES + t)
                picked[t + 1].append((member & (of_six | of_seven)).astype(F32))
        out_ref[s] = jnp.concatenate([a for p in picked for a in p], axis=0).astype(BF16)


def select_kernel(tokens_ref, picks_ref, out_ref):
    steps, _, half = tokens_ref.shape
    piece = half // (PIECES + 1)
    count = out_ref.shape[0]
    last, parts = None, [None] * PIECES
    for s in range(steps):
        one = dot(picks_ref[s, count:], tokens_ref[s, :, PIECES * piece :])
        last = one if last is None else last + one
        for t in range(PIECES):
            one = dot(picks_ref[s, :count], tokens_ref[s, :, t * piece : (t + 1) * piece])
            parts[t] = one if parts[t] is None else parts[t] + one
    for t in range(PIECES):
        out_ref[:, t * piece : (t + 1) * piece] = (
            parts[t] + last[t * count : (t + 1) * count]
        ).astype(BF16)


def load_kernel(*refs):
    count = (len(refs) - 2) // 2
    mark_ref, sems = refs[-2:]
    copies = []
    for i in range(count):
        rows = refs[i].shape[0] // LOADS
        for j in range(LOADS):
            part = pl.ds(j * rows, rows)
            copies.append(
                pltpu.make_async_copy(
                    refs[i].at[part], refs[count + i].at[part], sems.at[i * LOADS + j]
                )
            )
    for copy in copies:
        copy.start()
    mark_ref[...] = jnp.zeros_like(mark_ref)
    for copy in copies:
        copy.wait()


def pair_kernel(own_ref, came_ref, mark_ref, out_ref):
    del mark_ref
    both = jnp.concatenate([own_ref[...].astype(F32), came_ref[...].astype(F32)], axis=0)
    out_ref[...] = both.astype(BF16)


def load(*arrays):
    return call(
        load_kernel,
        [jax.ShapeDtypeStruct(a.shape, a.dtype) for a in arrays]
        + [jax.ShapeDtypeStruct((8, 128), F32)],
        *arrays,
        scratch=[pltpu.SemaphoreType.DMA((LOADS * len(arrays),))],
        here=range(len(arrays)),
        cost=sum(2 * a.size * a.dtype.itemsize for a in arrays),
        room=50 * MIB,
    )


def plan_kernel(flight, routes_ref, weights_ref, out_ref):
    steps, _, rows = routes_ref.shape
    lane = lax.broadcasted_iota(jnp.int32, (4 * 2 * PACK, rows), 0)
    block, place = lane // (2 * PACK), lane % PACK
    rest = jnp.where(place == SLOTS, block - 1, jnp.where(place == SLOTS + 1, PIECES + block - 1, -1))
    wanted = jnp.where(block == 0, jnp.where(place < SLOTS, place, -1), rest)
    for s in range(steps):
        routes, scale = routes_ref[s], weights_ref[s]
        for k in range(flight):
            member, slot = slots_of(routes, k, s)
            take = (member & (slot == wanted)).astype(F32)
            weight = jnp.sum(jnp.where(routes == k, scale, 0.0), axis=0, keepdims=True)
            both = jnp.concatenate([take, jnp.broadcast_to(weight, take.shape)], axis=0)
            out_ref[k, s * rows : (s + 1) * rows, :] = both.T


def gate_up_kernel(own_ref, one_ref, two_ref, three_ref, gate_ref, up_ref, out_ref):
    packed = own_ref.shape[1]
    piece = packed // PIECES
    hidden = gate_ref.shape[1]
    x = jnp.concatenate([r[...] for r in (own_ref, one_ref, two_ref, three_ref)], axis=0)
    rows = x.shape[0]
    tall = jnp.concatenate([x[:, t * piece : (t + 1) * piece] for t in range(PIECES)], axis=0)
    place = lax.broadcasted_iota(jnp.int32, (rows, hidden), 0) % PACK
    for h, ref in enumerate((gate_ref, up_ref)):
        total = dot(x, ref[:packed, :])
        last = dot(tall, ref[packed:, :])
        for t in range(PIECES):
            part = last[t * rows : (t + 1) * rows]
            low = pltpu.roll(part, rows - (SLOTS - t), 0)
            high = pltpu.roll(part, rows - (SLOTS + 1 - PIECES - t), 0)
            total = total + jnp.where(place == t, low, 0.0) + jnp.where(place == PIECES + t, high, 0.0)
        out_ref[:, h * hidden : (h + 1) * hidden] = total


def down_kernel(mine_ref, peer_ref, down_ref, *out_refs):
    rows = mine_ref.shape[0]
    depth = down_ref.shape[0]
    piece = down_ref.shape[1] // (PIECES + 1)
    total = mine_ref[...] + peer_ref[...]
    gate, up = total[:, :depth], total[:, depth:]
    hidden = (gate / (1.0 + jnp.exp(-gate)) * up).astype(BF16).astype(F32)
    place = lax.broadcasted_iota(jnp.int32, (rows, depth), 0) % PACK
    main = jnp.where(place < SLOTS, hidden, 0.0).astype(BF16)
    tall = jnp.concatenate(
        [
            jnp.where(place == SLOTS, pltpu.roll(hidden, SLOTS - t, 0), 0.0)
            + jnp.where(place == SLOTS + 1, pltpu.roll(hidden, SLOTS + 1 - PIECES - t, 0), 0.0)
            for t in range(PIECES)
        ],
        axis=0,
    ).astype(BF16)
    last = dot(tall, down_ref[:, PIECES * piece :])
    count = rows // len(out_refs)
    for t in range(PIECES):
        cols = slice(t * piece, (t + 1) * piece)
        part = (dot(main, down_ref[:, cols]) + last[t * rows : (t + 1) * rows]).astype(BF16)
        for b, ref in enumerate(out_refs):
            ref[:, cols] = part[b * count : (b + 1) * count]


def mix_kernel(flight, kept_ref, came_ref, plan_ref, out_ref, held, sems):
    packed = kept_ref.shape[1]
    piece = packed // PIECES
    value = kept_ref[...] + came_ref[...].astype(F32)
    upper = value.astype(BF16).astype(F32)
    lower = value - upper
    total = [None] * (PIECES + 1)
    for k in range(flight):
        weight = plan_ref[k, :, 4 * 2 * PACK : 4 * 2 * PACK + 1]
        main = plan_ref[k, :, : 2 * PACK].astype(BF16)
        rest = plan_ref[k, :, 2 * PACK : 4 * 2 * PACK].astype(BF16)
        take = slice(k * PACK, (k + 1) * PACK)
        both = jnp.concatenate([upper[take], lower[take]], axis=0).astype(BF16)
        tall = jnp.concatenate(
            [both[:, t * piece : (t + 1) * piece] for t in range(PIECES)], axis=0
        )
        for t in range(PIECES + 1):
            if t < PIECES:
                one = weight * dot(main, both[:, t * piece : (t + 1) * piece])
            else:
                one = weight * dot(rest, tall)
            total[t] = one if total[t] is None else total[t] + one
    copies = []
    for t in range(PIECES + 1):
        cols = pl.ds(t * piece, piece)
        held[:, t * piece : (t + 1) * piece] = total[t].astype(BF16)
        copies.append(pltpu.make_async_copy(held.at[:, cols], out_ref.at[:, cols], sems.at[t]))
        copies[-1].start()
    for copy in copies:
        copy.wait()


def local(tokens, routes, route_weights, gate_proj, up_proj, down_proj):
    steps, per_step, half = tokens.shape
    hidden_dev = gate_proj.shape[1]
    group = EF // hidden_dev
    devices = lax.axis_size("expert")
    flight = devices // group
    rows = steps * per_step
    packed = half // (PIECES + 1) * PIECES
    shape = jax.ShapeDtypeStruct
    routes = jnp.transpose(routes, (0, 2, 1))
    route_weights = jnp.transpose(route_weights, (0, 2, 1))

    def swap(x, mask):
        return lax.ppermute(x, "expert", [(i, i ^ mask) for i in range(devices)])

    def across(x):
        if flight == 1:
            return x
        places = [[p + group * b for b in range(flight)] for p in range(group)]
        return lax.all_to_all(x, "expert", 0, 0, axis_index_groups=places, tiled=True)

    count = flight * PACK
    picks = call(
        functools.partial(pick_kernel, flight),
        shape((steps, (PIECES + 1) * count, per_step), BF16),
        routes,
    )
    sent = call(select_kernel, shape((count, packed), BF16), tokens, picks)
    sent = across(sent)
    gate_proj, up_proj, mark = load(gate_proj, up_proj)
    plan = call(
        functools.partial(plan_kernel, flight),
        shape((flight, rows, 128), F32),
        routes,
        route_weights,
    )
    pair = call(pair_kernel, shape((2 * count, packed), BF16), sent, swap(sent, 4), mark)
    came = [swap(pair, mask) for mask in QUAD]
    all_rows = 8 * count
    products = call(
        gate_up_kernel,
        shape((all_rows, 2 * hidden_dev), F32),
        pair,
        *came,
        gate_proj,
        up_proj,
    )
    other = lax.ppermute(products, "attn", [(0, 1), (1, 0)])
    parts = call(
        down_kernel, [shape((2 * count, packed), BF16)] * 4, products, other, down_proj
    )
    back = [swap(part, mask) for part, mask in zip(parts[1:], QUAD)]
    summed = parts[0].astype(F32)
    for x in back:
        summed = summed + x.astype(F32)
    kept, away = summed[:count], summed[count:].astype(BF16)
    came_back = swap(away, 4)
    if flight > 1:
        kept = across((kept + came_back.astype(F32)).astype(BF16)).astype(F32)
        came_back = jnp.zeros_like(came_back)
    mixed = call(
        functools.partial(mix_kernel, flight),
        shape((rows, half), BF16),
        kept,
        came_back,
        plan,
        scratch=[pltpu.VMEM((rows, half), BF16), pltpu.SemaphoreType.DMA((PIECES + 1,))],
        out_here=True,
    )
    return mixed.reshape(steps, per_step, half)


def solution(mesh):
    in_specs = (
        P(None, ("groups", "expert"), "attn"),
        P(None, ("groups", "expert"), None),
        P(None, ("groups", "expert"), None),
        P("attn", "expert"),
        P("attn", "expert"),
        P("expert", "attn"),
    )
    out_specs = P(None, ("groups", "expert"), "attn")
    return jax.shard_map(local, mesh=mesh, in_specs=in_specs, out_specs=out_specs, check_vma=False)
```

time: 37.1 us -> 33.1 us (0.89)
  local copies, waits for them, and re-layouts: 4.98 us -> 1.84 us
  waiting for transfers between devices: 14.4 us -> 12.2 us
  Pallas kernels: 3.48 us -> 5.04 us
    unnamed x12 -> x10, local copies, waits for them, and re-layouts: 4.97 us -> 1.82 us
    ppermute x8, waiting for transfers between devices: 13.1 us -> 10.9 us  [swap(): return lax.ppermute(x, 'expert', [(i, i ^ mask) for i in range(devices)])]
    pallas_call x4 -> x8, Pallas kernels: 3.48 us -> 5.04 us  [call(): pl.pallas_call(kernel, out_shape=out_shape, in_specs=[hbm if i in here el...]
  transfers between devices with their start and end apart: 9 -> 9, of which waited for: 9 -> 9; matrix products, arithmetic and copies ran while one was open for 0% -> 0% of each run, Pallas kernels for 0% -> 7%
where the time goes in v2:
time: 33.1 us; the launch traced here: 32.8 us
  starting transfers between devices  13.6 us (41%)
  waiting for transfers between devices  12.2 us (37%)
  Pallas kernels  5.04 us (15%)
  local copies, waits for them, and re-layouts  1.84 us (6%)
    ppermute x8, starting transfers between devices, swap(): return lax.ppermute(x, 'expert', [(i, i ^ mask) for i in range(devices)])  13.6 us
    ppermute x8, waiting for transfers between devices, swap(): return lax.ppermute(x, 'expert', [(i, i ^ mask) for i in range(devices)])  10.9 us
    pallas_call x8, Pallas kernels, call(): pl.pallas_call(kernel, out_shape=out_shape, in_specs=[hbm if i in here el...  5.04 us
    unnamed x10, local copies, waits for them, and re-layouts  1.82 us
    ppermute x1, waiting for transfers between devices, local(): other = lax.ppermute(products, 'attn', [(0, 1), (1, 0)])  1.33 us
  transfers between devices with their start and end apart: 9, of which 9 were waited for; matrix products, arithmetic and copies ran while one was open for 0% of the time, Pallas kernels for 7%

profile of v2, /device:TPU:0, one launch (start us, length us, event | category | flops | bytes accessed | tf_op | source)
XLA Modules:
  0.0 32.8 jit_solution(14182880255023328727)
XLA Ops:
  0.0 0.0 copy-start.2
  0.0 0.7 %copy-done.2 = s32[3,32,8]{1,2,0:T(8,128)S(1)} copy-done((s32[3,32,8]{1,2,0:T(8,128)S(1)}, s32[3,32,8]{1,2,0:T(8,128)}, u32[]{:S(2)}) %copy-start.2) | copy-done | bytes 3096
  0.7 0.1 shard_map.64.picks_ref
  0.9 0.0 copy-start.1
  0.9 1.1 %copy-done.1 = bf16[3,32,3584]{2,1,0:T(8,128)(2,1)S(1)} copy-done((bf16[3,32,3584]{2,1,0:T(8,128)(2,1)S(1)}, bf16[3,32,3584]{2,1,0:T(8,128)(2,1)}, u32[]{:S(2)}) %copy-start.1) | copy-done | bytes 688152
  2.0 0.3 shard_map.65.own_ref
  2.2 4.1 %collective-permute-start = (bf16[8,2688]{1,0:T(8,128)(2,1)S(1)}, bf16[8,2688]{1,0:T(8,128)(2,1)S(1)}, u32[]{:S(2)}, u32[]{:S(2)}) collective-permute-start(bf16[8,2688]{1,0:T(8,128)(2,1)S(1)} %shard_map.65.own_ref), channel_id=1, source_target_pairs={{0,8},{2,10},{4,12},{6,14},{8,0},{10,2},{12,4},{14,6},{1,9},{3,11}... | collective-permute-start | bytes 129032 | tf_op jit(solution)/shard_map/ppermute | solution.py:229
  6.3 2.1 %shard_map.66 = (bf16[3584,256]{1,0:T(8,128)(2,1)S(1)}, bf16[3584,256]{1,0:T(8,128)(2,1)S(1)}, f32[8,128]{1,0:T(8,128)S(1)}) custom-call(bf16[3584,256]{1,0:T(8,128)(2,1)} %refs_0_.1, bf16[3584,256]{1,0:T(8,128)(2,1)} %refs_1_.1), custom_call_target="tpu_custom_call" | custom-call | bytes 7340032 | tf_op jit(solution)/shard_map/pallas_call | solution.py:26
  8.4 0.4 %collective-permute-done.came_ref = bf16[8,2688]{1,0:T(8,128)(2,1)S(1)} collective-permute-done((bf16[8,2688]{1,0:T(8,128)(2,1)S(1)}, bf16[8,2688]{1,0:T(8,128)(2,1)S(1)}, u32[]{:S(2)}, u32[]{:S(2)}) %collective-permute-start) | collective-permute-done | bytes 43040 | tf_op jit(solution)/shard_map/ppermute | solution.py:229
  8.8 2.4 %collective-permute-start.1 = (bf16[16,2688]{1,0:T(8,128)(2,1)S(1)}, bf16[16,2688]{1,0:T(8,128)(2,1)S(1)}, u32[]{:S(2)}, u32[]{:S(2)}) collective-permute-start(bf16[16,2688]{1,0:T(8,128)(2,1)S(1)} %shard_map.67.own_ref), channel_id=1, source_target_pairs={{0,6},{2,4},{4,2},{6,0},{8,14},{10,12},{12,10},{14,8},{1,7},{3,5},... | collective-permute-start | bytes 258056 | tf_op jit(solution)/shard_map/ppermute | solution.py:229
  11.2 0.8 %collective-permute-start.2 = (bf16[16,2688]{1,0:T(8,128)(2,1)S(1)}, bf16[16,2688]{1,0:T(8,128)(2,1)S(1)}, u32[]{:S(2)}, u32[]{:S(2)}) collective-permute-start(bf16[16,2688]{1,0:T(8,128)(2,1)S(1)} %shard_map.67.own_ref), channel_id=1, source_target_pairs={{0,4},{2,6},{4,0},{6,2},{8,12},{10,14},{12,8},{14,10},{1,5},{3,7},... | collective-permute-start | bytes 258056 | tf_op jit(solution)/shard_map/ppermute | solution.py:229
  12.0 0.3 collective-permute-start.3
  12.4 2.4 %collective-permute-done.1.one_ref = bf16[16,2688]{1,0:T(8,128)(2,1)S(1)} collective-permute-done((bf16[16,2688]{1,0:T(8,128)(2,1)S(1)}, bf16[16,2688]{1,0:T(8,128)(2,1)S(1)}, u32[]{:S(2)}, u32[]{:S(2)}) %collective-permute-start.1) | collective-permute-done | bytes 86048 | tf_op jit(solution)/shard_map/ppermute | solution.py:229
  14.7 1.0 %collective-permute-done.2.two_ref = bf16[16,2688]{1,0:T(8,128)(2,1)S(1)} collective-permute-done((bf16[16,2688]{1,0:T(8,128)(2,1)S(1)}, bf16[16,2688]{1,0:T(8,128)(2,1)S(1)}, u32[]{:S(2)}, u32[]{:S(2)}) %collective-permute-start.2) | collective-permute-done | bytes 86048 | tf_op jit(solution)/shard_map/ppermute | solution.py:229
  15.7 0.8 %collective-permute-done.3.three_ref = bf16[16,2688]{1,0:T(8,128)(2,1)S(1)} collective-permute-done((bf16[16,2688]{1,0:T(8,128)(2,1)S(1)}, bf16[16,2688]{1,0:T(8,128)(2,1)S(1)}, u32[]{:S(2)}, u32[]{:S(2)}) %collective-permute-start.3) | collective-permute-done | bytes 86048 | tf_op jit(solution)/shard_map/ppermute | solution.py:229
  16.5 0.0 copy-start
  16.5 0.8 %shard_map.68.mine_ref = f32[64,512]{1,0:T(8,128)S(1)} custom-call(bf16[16,2688]{1,0:T(8,128)(2,1)S(1)} %shard_map.67.own_ref, bf16[16,2688]{1,0:T(8,128)(2,1)S(1)} %collective-permute-done.1.one_ref, bf16[16,2688]{1,0:T(8,128)(2,1)S(1)} %collective-permute-done.2.two_ref, bf16[16,2688]{1,0:T(8,128)(2,1)S(1)} %collective-permute-done.3.three_ref, ...), custom_call_target="tpu_custom_call" | custom-call | tf_op jit(solution)/shard_map/pallas_call | solution.py:26
  17.3 0.0 copy-start.3
  17.3 0.0 copy-start.4
  17.4 0.1 collective-permute-start.4
  17.4 1.3 %collective-permute-done.4.peer_ref = f32[64,512]{1,0:T(8,128)S(1)} collective-permute-done((f32[64,512]{1,0:T(8,128)S(1)}, f32[64,512]{1,0:T(8,128)S(1)}, u32[]{:S(2)}, u32[]{:S(2)}) %collective-permute-start.4) | collective-permute-done | bytes 131104 | tf_op jit(solution)/shard_map/ppermute | solution.py:263
  18.8 0.0 copy-done
  18.8 0.5 %shard_map.69 = (bf16[16,2688]{1,0:T(8,128)(2,1)S(1)}, bf16[16,2688]{1,0:T(8,128)(2,1)S(1)}, bf16[16,2688]{1,0:T(8,128)(2,1)S(1)}, bf16[16,2688]{1,0:T(8,128)(2,1)S(1)}) custom-call(f32[64,512]{1,0:T(8,128)S(1)} %shard_map.68.mine_ref, f32[64,512]{1,0:T(8,128)S(1)} %collective-permute-done.4.peer_ref, bf16[256,3584]{1,0:T(8,128)(2,1)S(1)} %copy-done), custom_call_target="tpu_custom_call" | custom-call | tf_op jit(solution)/shard_map/pallas_call | solution.py:26
  19.3 1.3 %collective-permute-start.5 = (bf16[16,2688]{1,0:T(8,128)(2,1)S(1)}, bf16[16,2688]{1,0:T(8,128)(2,1)S(1)}, u32[]{:S(2)}, u32[]{:S(2)}) collective-permute-start(bf16[16,2688]{1,0:T(8,128)(2,1)S(1)} %get-tuple-element.16), channel_id=1, source_target_pairs={{0,6},{2,4},{4,2},{6,0},{8,14},{10,12},{12,10},{14,8},{1,7},{3,5},... | collective-permute-start | bytes 258056 | tf_op jit(solution)/shard_map/ppermute | solution.py:229
  20.5 0.8 %collective-permute-start.6 = (bf16[16,2688]{1,0:T(8,128)(2,1)S(1)}, bf16[16,2688]{1,0:T(8,128)(2,1)S(1)}, u32[]{:S(2)}, u32[]{:S(2)}) collective-permute-start(bf16[16,2688]{1,0:T(8,128)(2,1)S(1)} %get-tuple-element.17), channel_id=1, source_target_pairs={{0,4},{2,6},{4,0},{6,2},{8,12},{10,14},{12,8},{14,10},{1,5},{3,7},... | collective-permute-start | bytes 258056 | tf_op jit(solution)/shard_map/ppermute | solution.py:229
  21.4 1.5 %collective-permute-start.7 = (bf16[16,2688]{1,0:T(8,128)(2,1)S(1)}, bf16[16,2688]{1,0:T(8,128)(2,1)S(1)}, u32[]{:S(2)}, u32[]{:S(2)}) collective-permute-start(bf16[16,2688]{1,0:T(8,128)(2,1)S(1)} %get-tuple-element.18), channel_id=1, source_target_pairs={{0,2},{2,0},{4,6},{6,4},{8,10},{10,8},{12,14},{14,12},{1,3},{3,1},... | collective-permute-start | bytes 258056 | tf_op jit(solution)/shard_map/ppermute | solution.py:229
  22.8 2.8 %collective-permute-done.5 = bf16[16,2688]{1,0:T(8,128)(2,1)S(1)} collective-permute-done((bf16[16,2688]{1,0:T(8,128)(2,1)S(1)}, bf16[16,2688]{1,0:T(8,128)(2,1)S(1)}, u32[]{:S(2)}, u32[]{:S(2)}) %collective-permute-start.5) | collective-permute-done | bytes 86048 | tf_op jit(solution)/shard_map/ppermute | solution.py:229
  25.6 0.2 collective-permute-done.6
  25.8 0.9 %collective-permute-done.7 = bf16[16,2688]{1,0:T(8,128)(2,1)S(1)} collective-permute-done((bf16[16,2688]{1,0:T(8,128)(2,1)S(1)}, bf16[16,2688]{1,0:T(8,128)(2,1)S(1)}, u32[]{:S(2)}, u32[]{:S(2)}) %collective-permute-start.7) | collective-permute-done | bytes 86048 | tf_op jit(solution)/shard_map/ppermute | solution.py:229
  26.7 2.3 %collective-permute-start.8 = (bf16[8,2688]{1,0:T(8,128)(2,1)S(1)}, bf16[8,2688]{1,0:T(8,128)(2,1)S(1)}, u32[]{:S(2)}, u32[]{:S(2)}) collective-permute-start(bf16[8,2688]{1,0:T(8,128)(2,1)S(1)} %slice.12), channel_id=1, source_target_pairs={{0,8},{2,10},{4,12},{6,14},{8,0},{10,2},{12,4},{14,6},{1,9},{3,11}... | collective-permute-start | bytes 129032 | tf_op jit(solution)/shard_map/ppermute | solution.py:229
  29.1 0.0 copy-done.3
  29.1 0.0 copy-done.4
  29.1 0.2 shard_map.70.plan_ref
  29.3 2.5 %collective-permute-done.8.came_ref = bf16[8,2688]{1,0:T(8,128)(2,1)S(1)} collective-permute-done((bf16[8,2688]{1,0:T(8,128)(2,1)S(1)}, bf16[8,2688]{1,0:T(8,128)(2,1)S(1)}, u32[]{:S(2)}, u32[]{:S(2)}) %collective-permute-start.8) | collective-permute-done | bytes 43040 | tf_op jit(solution)/shard_map/ppermute | solution.py:229
  31.8 1.1 %shard_map.71 = bf16[96,3584]{1,0:T(8,128)(2,1)} custom-call(f32[8,2688]{1,0:T(8,128)S(1)} %slice.9.kept_ref, bf16[8,2688]{1,0:T(8,128)(2,1)S(1)} %collective-permute-done.8.came_ref, f32[1,96,128]{2,1,0:T(8,128)S(1)} %shard_map.70.plan_ref), custom_call_target="tpu_custom_call" | custom-call | tf_op jit(solution)/shard_map/pallas_call | solution.py:26
  (4 shorter events, 0.1 us)
Async XLA Ops:
  0.0 0.7 %copy-start.2 = (s32[3,32,8]{1,2,0:T(8,128)S(1)}, s32[3,32,8]{1,2,0:T(8,128)}, u32[]{:S(2)}) copy-start(s32[3,32,8]{1,2,0:T(8,128)} %param.7) | copy-start | bytes 9220
  0.9 1.1 %copy-start.1 = (bf16[3,32,3584]{2,1,0:T(8,128)(2,1)S(1)}, bf16[3,32,3584]{2,1,0:T(8,128)(2,1)}, u32[]{:S(2)}) copy-start(bf16[3,32,3584]{2,1,0:T(8,128)(2,1)} %tokens_ref.1) | copy-start | bytes 2064388
  2.2 6.6 %collective-permute-start = (bf16[8,2688]{1,0:T(8,128)(2,1)S(1)}, bf16[8,2688]{1,0:T(8,128)(2,1)S(1)}, u32[]{:S(2)}, u32[]{:S(2)}) collective-permute-start(bf16[8,2688]{1,0:T(8,128)(2,1)S(1)} %shard_map.65.own_ref), channel_id=1, source_target_pairs={{0,8},{2,10},{4,12},{6,14},{8,0},{10,2},{12,4},{14,6},{1,9},{3,11}... | collective-permute-start | bytes 129032 | tf_op jit(solution)/shard_map/ppermute | solution.py:229
  8.8 5.9 %collective-permute-start.1 = (bf16[16,2688]{1,0:T(8,128)(2,1)S(1)}, bf16[16,2688]{1,0:T(8,128)(2,1)S(1)}, u32[]{:S(2)}, u32[]{:S(2)}) collective-permute-start(bf16[16,2688]{1,0:T(8,128)(2,1)S(1)} %shard_map.67.own_ref), channel_id=1, source_target_pairs={{0,6},{2,4},{4,2},{6,0},{8,14},{10,12},{12,10},{14,8},{1,7},{3,5},... | collective-permute-start | bytes 258056 | tf_op jit(solution)/shard_map/ppermute | solution.py:229
  11.2 4.5 %collective-permute-start.2 = (bf16[16,2688]{1,0:T(8,128)(2,1)S(1)}, bf16[16,2688]{1,0:T(8,128)(2,1)S(1)}, u32[]{:S(2)}, u32[]{:S(2)}) collective-permute-start(bf16[16,2688]{1,0:T(8,128)(2,1)S(1)} %shard_map.67.own_ref), channel_id=1, source_target_pairs={{0,4},{2,6},{4,0},{6,2},{8,12},{10,14},{12,8},{14,10},{1,5},{3,7},... | collective-permute-start | bytes 258056 | tf_op jit(solution)/shard_map/ppermute | solution.py:229
  12.0 4.5 %collective-permute-start.3 = (bf16[16,2688]{1,0:T(8,128)(2,1)S(1)}, bf16[16,2688]{1,0:T(8,128)(2,1)S(1)}, u32[]{:S(2)}, u32[]{:S(2)}) collective-permute-start(bf16[16,2688]{1,0:T(8,128)(2,1)S(1)} %shard_map.67.own_ref), channel_id=1, source_target_pairs={{0,2},{2,0},{4,6},{6,4},{8,10},{10,8},{12,14},{14,12},{1,3},{3,1},... | collective-permute-start | bytes 258056 | tf_op jit(solution)/shard_map/ppermute | solution.py:229
  16.5 2.3 %copy-start = (bf16[256,3584]{1,0:T(8,128)(2,1)S(1)}, bf16[256,3584]{1,0:T(8,128)(2,1)}, u32[]{:S(2)}) copy-start(bf16[256,3584]{1,0:T(8,128)(2,1)} %down_ref.1) | copy-start | bytes 5505028
  17.3 11.7 %copy-start.3 = (s32[3,32,8]{1,2,0:T(8,128)S(1)}, s32[3,32,8]{1,2,0:T(8,128)}, u32[]{:S(2)}) copy-start(s32[3,32,8]{1,2,0:T(8,128)} %param.7) | copy-start | bytes 9220
  17.3 11.7 %copy-start.4 = (f32[3,32,8]{1,2,0:T(8,128)S(1)}, f32[3,32,8]{1,2,0:T(8,128)}, u32[]{:S(2)}) copy-start(f32[3,32,8]{1,2,0:T(8,128)} %param.8) | copy-start | bytes 9220
  17.4 1.4 %collective-permute-start.4 = (f32[64,512]{1,0:T(8,128)S(1)}, f32[64,512]{1,0:T(8,128)S(1)}, u32[]{:S(2)}, u32[]{:S(2)}) collective-permute-start(f32[64,512]{1,0:T(8,128)S(1)} %shard_map.68.mine_ref), channel_id=1, source_target_pairs={{0,1},{1,0},{2,3},{3,2},{4,5},{5,4},{6,7},{7,6},{8,9},{9,8},{10,11... | collective-permute-start | bytes 393224 | tf_op jit(solution)/shard_map/ppermute | solution.py:263
  19.3 6.3 %collective-permute-start.5 = (bf16[16,2688]{1,0:T(8,128)(2,1)S(1)}, bf16[16,2688]{1,0:T(8,128)(2,1)S(1)}, u32[]{:S(2)}, u32[]{:S(2)}) collective-permute-start(bf16[16,2688]{1,0:T(8,128)(2,1)S(1)} %get-tuple-element.16), channel_id=1, source_target_pairs={{0,6},{2,4},{4,2},{6,0},{8,14},{10,12},{12,10},{14,8},{1,7},{3,5},... | collective-permute-start | bytes 258056 | tf_op jit(solution)/shard_map/ppermute | solution.py:229
  20.5 5.2 %collective-permute-start.6 = (bf16[16,2688]{1,0:T(8,128)(2,1)S(1)}, bf16[16,2688]{1,0:T(8,128)(2,1)S(1)}, u32[]{:S(2)}, u32[]{:S(2)}) collective-permute-start(bf16[16,2688]{1,0:T(8,128)(2,1)S(1)} %get-tuple-element.17), channel_id=1, source_target_pairs={{0,4},{2,6},{4,0},{6,2},{8,12},{10,14},{12,8},{14,10},{1,5},{3,7},... | collective-permute-start | bytes 258056 | tf_op jit(solution)/shard_map/ppermute | solution.py:229
  21.4 5.3 %collective-permute-start.7 = (bf16[16,2688]{1,0:T(8,128)(2,1)S(1)}, bf16[16,2688]{1,0:T(8,128)(2,1)S(1)}, u32[]{:S(2)}, u32[]{:S(2)}) collective-permute-start(bf16[16,2688]{1,0:T(8,128)(2,1)S(1)} %get-tuple-element.18), channel_id=1, source_target_pairs={{0,2},{2,0},{4,6},{6,4},{8,10},{10,8},{12,14},{14,12},{1,3},{3,1},... | collective-permute-start | bytes 258056 | tf_op jit(solution)/shard_map/ppermute | solution.py:229
  26.7 5.1 %collective-permute-start.8 = (bf16[8,2688]{1,0:T(8,128)(2,1)S(1)}, bf16[8,2688]{1,0:T(8,128)(2,1)S(1)}, u32[]{:S(2)}, u32[]{:S(2)}) collective-permute-start(bf16[8,2688]{1,0:T(8,128)(2,1)S(1)} %slice.12), channel_id=1, source_target_pairs={{0,8},{2,10},{4,12},{6,14},{8,0},{10,2},{12,4},{14,6},{1,9},{3,11}... | collective-permute-start | bytes 129032 | tf_op jit(solution)/shard_map/ppermute | solution.py:229

commit v3 on v2

--- a/solution.py
+++ b/solution.py
@@ -13,6 +13,7 @@
 SLOTS = STEPS * CAP
 PACK = 8
 PIECES = 3
+SENT = 7
 QUAD = (3, 2, 1)
 LOADS = 4
 MIB = 1024 * 1024
@@ -48,37 +49,48 @@
     return member > 0.5, step * CAP + before
 
 
-def pick_kernel(flight, routes_ref, out_ref):
-    steps, _, rows = routes_ref.shape
+def select_kernel(flight, tokens_ref, routes_ref, *refs):
+    out_refs, (held, chosen, sems) = refs[:-3], refs[-3:]
+    steps, rows, half = tokens_ref.shape
+    piece = half // (PIECES + 1)
+    copies = [
+        pltpu.make_async_copy(tokens_ref.at[s], held.at[s], sems.at[s]) for s in range(steps)
+    ]
+    routes_copy = pltpu.make_async_copy(routes_ref, chosen, sems.at[steps])
+    routes_copy.start()
+    for copy in copies:
+        copy.start()
+    routes_copy.wait()
     place = lax.broadcasted_iota(jnp.int32, (PACK, rows), 0)
+    mains, rests = [], []
     for s in range(steps):
-        routes = routes_ref[s]
-        picked = [[] for _ in range(PIECES + 1)]
+        routes = chosen[s]
+        main, rest = [], [[] for _ in range(PIECES)]
         for k in range(flight):
             member, slot = slots_of(routes, k, s)
-            picked[0].append((member & (slot == place)).astype(F32))
+            main.append((member & (slot == place)).astype(BF16))
             for t in range(PIECES):
                 of_six = (place == SLOTS) & (slot == t)
                 of_seven = (place == SLOTS + 1) & (slot == PIECES + t)
-                picked[t + 1].append((member & (of_six | of_seven)).astype(F32))
-        out_ref[s] = jnp.concatenate([a for p in picked for a in p], axis=0).astype(BF16)
-
-
-def select_kernel(tokens_ref, picks_ref, out_ref):
-    steps, _, half = tokens_ref.shape
-    piece = half // (PIECES + 1)
-    count = out_ref.shape[0]
+                rest[t].append((member & (of_six | of_seven)).astype(BF16))
+        mains.append(jnp.concatenate(main, axis=0))
+        rests.append(jnp.concatenate([a for t in rest for a in t], axis=0))
+    count = flight * PACK
     last, parts = None, [None] * PIECES
     for s in range(steps):
-        one = dot(picks_ref[s, count:], tokens_ref[s, :, PIECES * piece :])
+        copies[s].wait()
+        one = dot(rests[s], held[s, :, PIECES * piece :])
         last = one if last is None else last + one
         for t in range(PIECES):
-            one = dot(picks_ref[s, :count], tokens_ref[s, :, t * piece : (t + 1) * piece])
+            one = dot(mains[s], held[s, :, t * piece : (t + 1) * piece])
             parts[t] = one if parts[t] is None else parts[t] + one
-    for t in range(PIECES):
-        out_ref[:, t * piece : (t + 1) * piece] = (
-            parts[t] + last[t * count : (t + 1) * count]
-        ).astype(BF16)
+    whole = jnp.concatenate(
+        [parts[t] + last[t * count : (t + 1) * count] for t in range(PIECES)], axis=1
+    ).astype(BF16)
+    start = 0
+    for ref in out_refs:
+        ref[...] = whole[:, start : start + ref.shape[1]]
+        start += ref.shape[1]
 
 
 def load_kernel(*refs):
@@ -120,8 +132,16 @@
     )
 
 
-def plan_kernel(flight, routes_ref, weights_ref, out_ref):
+def plan_kernel(flight, routes_hbm, weights_hbm, out_ref, routes_ref, weights_ref, sems):
     steps, _, rows = routes_ref.shape
+    copies = [
+        pltpu.make_async_copy(routes_hbm, routes_ref, sems.at[0]),
+        pltpu.make_async_copy(weights_hbm, weights_ref, sems.at[1]),
+    ]
+    for copy in copies:
+        copy.start()
+    for copy in copies:
+        copy.wait()
     lane = lax.broadcasted_iota(jnp.int32, (4 * 2 * PACK, rows), 0)
     block, place = lane // (2 * PACK), lane % PACK
     rest = jnp.where(place == SLOTS, block - 1, jnp.where(place == SLOTS + 1, PIECES + block - 1, -1))
@@ -235,44 +255,66 @@
         return lax.all_to_all(x, "expert", 0, 0, axis_index_groups=places, tiled=True)
 
     count = flight * PACK
-    picks = call(
-        functools.partial(pick_kernel, flight),
-        shape((steps, (PIECES + 1) * count, per_step), BF16),
+    sent = call(
+        functools.partial(select_kernel, flight),
+        [shape((count, packed // SENT), BF16)] * SENT,
+        tokens,
         routes,
-    )
-    sent = call(select_kernel, shape((count, packed), BF16), tokens, picks)
-    sent = across(sent)
+        scratch=[
+            pltpu.VMEM(tokens.shape, BF16),
+            pltpu.VMEM(routes.shape, jnp.int32),
+            pltpu.SemaphoreType.DMA((steps + 1,)),
+        ],
+        here=(0, 1),
+        room=55169 * 1024,
+    )
+    sent = across(jnp.concatenate(sent, axis=1))
     gate_proj, up_proj, mark = load(gate_proj, up_proj)
     plan = call(
         functools.partial(plan_kernel, flight),
         shape((flight, rows, 128), F32),
         routes,
         route_weights,
-    )
-    pair = call(pair_kernel, shape((2 * count, packed), BF16), sent, swap(sent, 4), mark)
-    came = [swap(pair, mask) for mask in QUAD]
-    all_rows = 8 * count
+        scratch=[
+            pltpu.VMEM(routes.shape, jnp.int32),
+            pltpu.VMEM(route_weights.shape, F32),
+            pltpu.SemaphoreType.DMA((2,)),
+        ],
+        here=(0, 1),
+    )
+    high = [bit for bit in (group >> n for n in range(1, group.bit_length())) if bit >= 4]
+    block = sent
+    for bit in high:
+        block = call(
+            pair_kernel,
+            shape((2 * block.shape[0], packed), BF16),
+            block,
+            swap(block, bit),
+            mark,
+        )
+    came = [swap(block, mask) for mask in QUAD]
     products = call(
         gate_up_kernel,
-        shape((all_rows, 2 * hidden_dev), F32),
-        pair,
+        shape((group * count, 2 * hidden_dev), F32),
+        block,
         *came,
         gate_proj,
         up_proj,
     )
     other = lax.ppermute(products, "attn", [(0, 1), (1, 0)])
-    parts = call(
-        down_kernel, [shape((2 * count, packed), BF16)] * 4, products, other, down_proj
-    )
+    parts = call(down_kernel, [shape(block.shape, BF16)] * 4, products, other, down_proj)
     back = [swap(part, mask) for part, mask in zip(parts[1:], QUAD)]
     summed = parts[0].astype(F32)
     for x in back:
         summed = summed + x.astype(F32)
-    kept, away = summed[:count], summed[count:].astype(BF16)
-    came_back = swap(away, 4)
+    for bit in reversed(high):
+        half_rows = summed.shape[0] // 2
+        kept, away = summed[:half_rows], summed[half_rows:].astype(BF16)
+        came_back = swap(away, bit)
+        summed = kept + came_back.astype(F32)
     if flight > 1:
-        kept = across((kept + came_back.astype(F32)).astype(BF16)).astype(F32)
-        came_back = jnp.zeros_like(came_back)
+        kept = across(summed.astype(BF16)).astype(F32)
+        came_back = jnp.zeros(kept.shape, BF16)
     mixed = call(
         functools.partial(mix_kernel, flight),
         shape((rows, half), BF16),

time: 33.1 us -> 32.4 us (0.979)
  local copies, waits for them, and re-layouts: 1.84 us -> 0.09 us
  Pallas kernels: 5.04 us -> 6.17 us
    unnamed x10 -> x12, local copies, waits for them, and re-layouts: 1.82 us -> 0.06 us
    pallas_call x8 -> x7, Pallas kernels: 5.04 us -> 6.17 us  [call(): pl.pallas_call(kernel, out_shape=out_shape, in_specs=[hbm if i in here el...]
where the time goes in v3:
time: 32.4 us; the launch traced here: 32.2 us
  starting transfers between devices  13.6 us (42%)
  waiting for transfers between devices  12.2 us (38%)
  Pallas kernels  6.17 us (19%)
    ppermute x8, starting transfers between devices, swap(): return lax.ppermute(x, 'expert', [(i, i ^ mask) for i in range(devices)])  13.6 us
    ppermute x8, waiting for transfers between devices, swap(): return lax.ppermute(x, 'expert', [(i, i ^ mask) for i in range(devices)])  10.8 us
    pallas_call x7, Pallas kernels, call(): pl.pallas_call(kernel, out_shape=out_shape, in_specs=[hbm if i in here el...  6.17 us
    ppermute x1, waiting for transfers between devices, local(): other = lax.ppermute(products, 'attn', [(0, 1), (1, 0)])  1.33 us
  transfers between devices with their start and end apart: 9, of which 9 were waited for; matrix products, arithmetic and copies ran while one was open for 0% of the time, Pallas kernels for 7%

profile of v3, /device:TPU:0, one launch (start us, length us, event | category | flops | bytes accessed | tf_op | source)
XLA Modules:
  0.0 32.2 jit_solution(9171810891727624351)
XLA Ops:
  0.0 1.5 %shard_map.64 = (bf16[8,384]{1,0:T(8,128)(2,1)S(1)}, bf16[8,384]{1,0:T(8,128)(2,1)S(1)}, bf16[8,384]{1,0:T(8,128)(2,1)S(1)}, bf16[8,384]{1,0:T(8,128)(2,1)S(1)},...) custom-call(bf16[3,32,3584]{2,1,0:T(8,128)(2,1)} %tokens_ref.1, ...), custom_call_target="tpu_custom_call" | custom-call | tf_op jit(solution)/shard_map/pallas_call | solution.py:27
  1.6 4.1 %collective-permute-start = (bf16[8,2688]{1,0:T(8,128)(2,1)S(1)}, bf16[8,2688]{1,0:T(8,128)(2,1)S(1)}, u32[]{:S(2)}, u32[]{:S(2)}) collective-permute-start(bf16[8,2688]{1,0:T(8,128)(2,1)S(1)} %constant_dynamic-update-slice_fusion.own_ref), channel_id=1, source_target_pairs={{0,8},{2,10},{4,12},{6,14},{8,0},{10,2},{12,4},{14,6},{1,9},{3,11}... | collective-permute-start | bytes 129032 | tf_op jit(solution)/shard_map/ppermute | solution.py:249
  5.7 2.1 %shard_map.65 = (bf16[3584,256]{1,0:T(8,128)(2,1)S(1)}, bf16[3584,256]{1,0:T(8,128)(2,1)S(1)}, f32[8,128]{1,0:T(8,128)S(1)}) custom-call(bf16[3584,256]{1,0:T(8,128)(2,1)} %refs_0_.1, bf16[3584,256]{1,0:T(8,128)(2,1)} %refs_1_.1), custom_call_target="tpu_custom_call" | custom-call | bytes 7340032 | tf_op jit(solution)/shard_map/pallas_call | solution.py:27
  7.8 0.4 %collective-permute-done.came_ref = bf16[8,2688]{1,0:T(8,128)(2,1)S(1)} collective-permute-done((bf16[8,2688]{1,0:T(8,128)(2,1)S(1)}, bf16[8,2688]{1,0:T(8,128)(2,1)S(1)}, u32[]{:S(2)}, u32[]{:S(2)}) %collective-permute-start) | collective-permute-done | bytes 43040 | tf_op jit(solution)/shard_map/ppermute | solution.py:249
  8.2 2.4 %collective-permute-start.1 = (bf16[16,2688]{1,0:T(8,128)(2,1)S(1)}, bf16[16,2688]{1,0:T(8,128)(2,1)S(1)}, u32[]{:S(2)}, u32[]{:S(2)}) collective-permute-start(bf16[16,2688]{1,0:T(8,128)(2,1)S(1)} %shard_map.66.own_ref), channel_id=1, source_target_pairs={{0,6},{2,4},{4,2},{6,0},{8,14},{10,12},{12,10},{14,8},{1,7},{3,5},... | collective-permute-start | bytes 258056 | tf_op jit(solution)/shard_map/ppermute | solution.py:249
  10.6 0.8 %collective-permute-start.2 = (bf16[16,2688]{1,0:T(8,128)(2,1)S(1)}, bf16[16,2688]{1,0:T(8,128)(2,1)S(1)}, u32[]{:S(2)}, u32[]{:S(2)}) collective-permute-start(bf16[16,2688]{1,0:T(8,128)(2,1)S(1)} %shard_map.66.own_ref), channel_id=1, source_target_pairs={{0,4},{2,6},{4,0},{6,2},{8,12},{10,14},{12,8},{14,10},{1,5},{3,7},... | collective-permute-start | bytes 258056 | tf_op jit(solution)/shard_map/ppermute | solution.py:249
  11.4 0.3 %collective-permute-start.3 = (bf16[16,2688]{1,0:T(8,128)(2,1)S(1)}, bf16[16,2688]{1,0:T(8,128)(2,1)S(1)}, u32[]{:S(2)}, u32[]{:S(2)}) collective-permute-start(bf16[16,2688]{1,0:T(8,128)(2,1)S(1)} %shard_map.66.own_ref), channel_id=1, source_target_pairs={{0,2},{2,0},{4,6},{6,4},{8,10},{10,8},{12,14},{14,12},{1,3},{3,1},... | collective-permute-start | bytes 258056 | tf_op jit(solution)/shard_map/ppermute | solution.py:249
  11.7 2.4 %collective-permute-done.1.one_ref = bf16[16,2688]{1,0:T(8,128)(2,1)S(1)} collective-permute-done((bf16[16,2688]{1,0:T(8,128)(2,1)S(1)}, bf16[16,2688]{1,0:T(8,128)(2,1)S(1)}, u32[]{:S(2)}, u32[]{:S(2)}) %collective-permute-start.1) | collective-permute-done | bytes 86048 | tf_op jit(solution)/shard_map/ppermute | solution.py:249
  14.1 1.0 %collective-permute-done.2.two_ref = bf16[16,2688]{1,0:T(8,128)(2,1)S(1)} collective-permute-done((bf16[16,2688]{1,0:T(8,128)(2,1)S(1)}, bf16[16,2688]{1,0:T(8,128)(2,1)S(1)}, u32[]{:S(2)}, u32[]{:S(2)}) %collective-permute-start.2) | collective-permute-done | bytes 86048 | tf_op jit(solution)/shard_map/ppermute | solution.py:249
  15.1 0.8 %collective-permute-done.3.three_ref = bf16[16,2688]{1,0:T(8,128)(2,1)S(1)} collective-permute-done((bf16[16,2688]{1,0:T(8,128)(2,1)S(1)}, bf16[16,2688]{1,0:T(8,128)(2,1)S(1)}, u32[]{:S(2)}, u32[]{:S(2)}) %collective-permute-start.3) | collective-permute-done | bytes 86048 | tf_op jit(solution)/shard_map/ppermute | solution.py:249
  15.9 0.0 copy-start
  15.9 0.8 %shard_map.67.mine_ref = f32[64,512]{1,0:T(8,128)S(1)} custom-call(bf16[16,2688]{1,0:T(8,128)(2,1)S(1)} %shard_map.66.own_ref, bf16[16,2688]{1,0:T(8,128)(2,1)S(1)} %collective-permute-done.1.one_ref, bf16[16,2688]{1,0:T(8,128)(2,1)S(1)} %collective-permute-done.2.two_ref, bf16[16,2688]{1,0:T(8,128)(2,1)S(1)} %collective-permute-done.3.three_ref, ...), custom_call_target="tpu_custom_call" | custom-call | tf_op jit(solution)/shard_map/pallas_call | solution.py:27
  16.7 0.0 copy-start.1
  16.7 0.0 copy-start.2
  16.7 0.1 collective-permute-start.4
  16.8 1.3 %collective-permute-done.4.peer_ref = f32[64,512]{1,0:T(8,128)S(1)} collective-permute-done((f32[64,512]{1,0:T(8,128)S(1)}, f32[64,512]{1,0:T(8,128)S(1)}, u32[]{:S(2)}, u32[]{:S(2)}) %collective-permute-start.4) | collective-permute-done | bytes 131104 | tf_op jit(solution)/shard_map/ppermute | solution.py:304
  18.1 0.0 copy-done
  18.1 0.5 %shard_map.68 = (bf16[16,2688]{1,0:T(8,128)(2,1)S(1)}, bf16[16,2688]{1,0:T(8,128)(2,1)S(1)}, bf16[16,2688]{1,0:T(8,128)(2,1)S(1)}, bf16[16,2688]{1,0:T(8,128)(2,1)S(1)}) custom-call(f32[64,512]{1,0:T(8,128)S(1)} %shard_map.67.mine_ref, f32[64,512]{1,0:T(8,128)S(1)} %collective-permute-done.4.peer_ref, bf16[256,3584]{1,0:T(8,128)(2,1)S(1)} %copy-done), custom_call_target="tpu_custom_call" | custom-call | tf_op jit(solution)/shard_map/pallas_call | solution.py:27
  18.6 1.3 %collective-permute-start.5 = (bf16[16,2688]{1,0:T(8,128)(2,1)S(1)}, bf16[16,2688]{1,0:T(8,128)(2,1)S(1)}, u32[]{:S(2)}, u32[]{:S(2)}) collective-permute-start(bf16[16,2688]{1,0:T(8,128)(2,1)S(1)} %get-tuple-element.30), channel_id=1, source_target_pairs={{0,6},{2,4},{4,2},{6,0},{8,14},{10,12},{12,10},{14,8},{1,7},{3,5},... | collective-permute-start | bytes 258056 | tf_op jit(solution)/shard_map/ppermute | solution.py:249
  19.9 0.8 %collective-permute-start.6 = (bf16[16,2688]{1,0:T(8,128)(2,1)S(1)}, bf16[16,2688]{1,0:T(8,128)(2,1)S(1)}, u32[]{:S(2)}, u32[]{:S(2)}) collective-permute-start(bf16[16,2688]{1,0:T(8,128)(2,1)S(1)} %get-tuple-element.31), channel_id=1, source_target_pairs={{0,4},{2,6},{4,0},{6,2},{8,12},{10,14},{12,8},{14,10},{1,5},{3,7},... | collective-permute-start | bytes 258056 | tf_op jit(solution)/shard_map/ppermute | solution.py:249
  20.7 1.5 %collective-permute-start.7 = (bf16[16,2688]{1,0:T(8,128)(2,1)S(1)}, bf16[16,2688]{1,0:T(8,128)(2,1)S(1)}, u32[]{:S(2)}, u32[]{:S(2)}) collective-permute-start(bf16[16,2688]{1,0:T(8,128)(2,1)S(1)} %get-tuple-element.32), channel_id=1, source_target_pairs={{0,2},{2,0},{4,6},{6,4},{8,10},{10,8},{12,14},{14,12},{1,3},{3,1},... | collective-permute-start | bytes 258056 | tf_op jit(solution)/shard_map/ppermute | solution.py:249
  22.2 2.8 %collective-permute-done.5 = bf16[16,2688]{1,0:T(8,128)(2,1)S(1)} collective-permute-done((bf16[16,2688]{1,0:T(8,128)(2,1)S(1)}, bf16[16,2688]{1,0:T(8,128)(2,1)S(1)}, u32[]{:S(2)}, u32[]{:S(2)}) %collective-permute-start.5) | collective-permute-done | bytes 86048 | tf_op jit(solution)/shard_map/ppermute | solution.py:249
  24.9 0.2 collective-permute-done.6
  25.1 0.9 %collective-permute-done.7 = bf16[16,2688]{1,0:T(8,128)(2,1)S(1)} collective-permute-done((bf16[16,2688]{1,0:T(8,128)(2,1)S(1)}, bf16[16,2688]{1,0:T(8,128)(2,1)S(1)}, u32[]{:S(2)}, u32[]{:S(2)}) %collective-permute-start.7) | collective-permute-done | bytes 86048 | tf_op jit(solution)/shard_map/ppermute | solution.py:249
  26.1 2.3 %collective-permute-start.8 = (bf16[8,2688]{1,0:T(8,128)(2,1)S(1)}, bf16[8,2688]{1,0:T(8,128)(2,1)S(1)}, u32[]{:S(2)}, u32[]{:S(2)}) collective-permute-start(bf16[8,2688]{1,0:T(8,128)(2,1)S(1)} %slice.12), channel_id=1, source_target_pairs={{0,8},{2,10},{4,12},{6,14},{8,0},{10,2},{12,4},{14,6},{1,9},{3,11}... | collective-permute-start | bytes 129032 | tf_op jit(solution)/shard_map/ppermute | solution.py:249
  28.4 0.0 copy-done.1
  28.4 0.0 copy-done.2
  28.4 0.3 shard_map.69.plan_ref
  28.7 2.4 %collective-permute-done.8.came_ref = bf16[8,2688]{1,0:T(8,128)(2,1)S(1)} collective-permute-done((bf16[8,2688]{1,0:T(8,128)(2,1)S(1)}, bf16[8,2688]{1,0:T(8,128)(2,1)S(1)}, u32[]{:S(2)}, u32[]{:S(2)}) %collective-permute-start.8) | collective-permute-done | bytes 43040 | tf_op jit(solution)/shard_map/ppermute | solution.py:249
  31.1 1.1 %shard_map.70 = bf16[96,3584]{1,0:T(8,128)(2,1)} custom-call(f32[8,2688]{1,0:T(8,128)S(1)} %slice.9.kept_ref, bf16[8,2688]{1,0:T(8,128)(2,1)S(1)} %collective-permute-done.8.came_ref, f32[1,96,128]{2,1,0:T(8,128)S(1)} %shard_map.69.plan_ref), custom_call_target="tpu_custom_call" | custom-call | tf_op jit(solution)/shard_map/pallas_call | solution.py:27
  (11 shorter events, 0.1 us)
Async XLA Ops:
  1.6 6.6 %collective-permute-start = (bf16[8,2688]{1,0:T(8,128)(2,1)S(1)}, bf16[8,2688]{1,0:T(8,128)(2,1)S(1)}, u32[]{:S(2)}, u32[]{:S(2)}) collective-permute-start(bf16[8,2688]{1,0:T(8,128)(2,1)S(1)} %constant_dynamic-update-slice_fusion.own_ref), channel_id=1, source_target_pairs={{0,8},{2,10},{4,12},{6,14},{8,0},{10,2},{12,4},{14,6},{1,9},{3,11}... | collective-permute-start | bytes 129032 | tf_op jit(solution)/shard_map/ppermute | solution.py:249
  8.2 5.9 %collective-permute-start.1 = (bf16[16,2688]{1,0:T(8,128)(2,1)S(1)}, bf16[16,2688]{1,0:T(8,128)(2,1)S(1)}, u32[]{:S(2)}, u32[]{:S(2)}) collective-permute-start(bf16[16,2688]{1,0:T(8,128)(2,1)S(1)} %shard_map.66.own_ref), channel_id=1, source_target_pairs={{0,6},{2,4},{4,2},{6,0},{8,14},{10,12},{12,10},{14,8},{1,7},{3,5},... | collective-permute-start | bytes 258056 | tf_op jit(solution)/shard_map/ppermute | solution.py:249
  10.6 4.5 %collective-permute-start.2 = (bf16[16,2688]{1,0:T(8,128)(2,1)S(1)}, bf16[16,2688]{1,0:T(8,128)(2,1)S(1)}, u32[]{:S(2)}, u32[]{:S(2)}) collective-permute-start(bf16[16,2688]{1,0:T(8,128)(2,1)S(1)} %shard_map.66.own_ref), channel_id=1, source_target_pairs={{0,4},{2,6},{4,0},{6,2},{8,12},{10,14},{12,8},{14,10},{1,5},{3,7},... | collective-permute-start | bytes 258056 | tf_op jit(solution)/shard_map/ppermute | solution.py:249
  11.4 4.5 %collective-permute-start.3 = (bf16[16,2688]{1,0:T(8,128)(2,1)S(1)}, bf16[16,2688]{1,0:T(8,128)(2,1)S(1)}, u32[]{:S(2)}, u32[]{:S(2)}) collective-permute-start(bf16[16,2688]{1,0:T(8,128)(2,1)S(1)} %shard_map.66.own_ref), channel_id=1, source_target_pairs={{0,2},{2,0},{4,6},{6,4},{8,10},{10,8},{12,14},{14,12},{1,3},{3,1},... | collective-permute-start | bytes 258056 | tf_op jit(solution)/shard_map/ppermute | solution.py:249
  15.9 2.3 %copy-start = (bf16[256,3584]{1,0:T(8,128)(2,1)S(1)}, bf16[256,3584]{1,0:T(8,128)(2,1)}, u32[]{:S(2)}) copy-start(bf16[256,3584]{1,0:T(8,128)(2,1)} %down_ref.1) | copy-start | bytes 5505028
  16.7 11.7 %copy-start.1 = (s32[3,32,8]{1,2,0:T(8,128)S(1)}, s32[3,32,8]{1,2,0:T(8,128)}, u32[]{:S(2)}) copy-start(s32[3,32,8]{1,2,0:T(8,128)} %param.7) | copy-start | bytes 9220
  16.7 11.7 %copy-start.2 = (f32[3,32,8]{1,2,0:T(8,128)S(1)}, f32[3,32,8]{1,2,0:T(8,128)}, u32[]{:S(2)}) copy-start(f32[3,32,8]{1,2,0:T(8,128)} %param.8) | copy-start | bytes 9220
  16.7 1.4 %collective-permute-start.4 = (f32[64,512]{1,0:T(8,128)S(1)}, f32[64,512]{1,0:T(8,128)S(1)}, u32[]{:S(2)}, u32[]{:S(2)}) collective-permute-start(f32[64,512]{1,0:T(8,128)S(1)} %shard_map.67.mine_ref), channel_id=1, source_target_pairs={{0,1},{1,0},{2,3},{3,2},{4,5},{5,4},{6,7},{7,6},{8,9},{9,8},{10,11... | collective-permute-start | bytes 393224 | tf_op jit(solution)/shard_map/ppermute | solution.py:304
  18.6 6.3 %collective-permute-start.5 = (bf16[16,2688]{1,0:T(8,128)(2,1)S(1)}, bf16[16,2688]{1,0:T(8,128)(2,1)S(1)}, u32[]{:S(2)}, u32[]{:S(2)}) collective-permute-start(bf16[16,2688]{1,0:T(8,128)(2,1)S(1)} %get-tuple-element.30), channel_id=1, source_target_pairs={{0,6},{2,4},{4,2},{6,0},{8,14},{10,12},{12,10},{14,8},{1,7},{3,5},... | collective-permute-start | bytes 258056 | tf_op jit(solution)/shard_map/ppermute | solution.py:249
  19.9 5.2 %collective-permute-start.6 = (bf16[16,2688]{1,0:T(8,128)(2,1)S(1)}, bf16[16,2688]{1,0:T(8,128)(2,1)S(1)}, u32[]{:S(2)}, u32[]{:S(2)}) collective-permute-start(bf16[16,2688]{1,0:T(8,128)(2,1)S(1)} %get-tuple-element.31), channel_id=1, source_target_pairs={{0,4},{2,6},{4,0},{6,2},{8,12},{10,14},{12,8},{14,10},{1,5},{3,7},... | collective-permute-start | bytes 258056 | tf_op jit(solution)/shard_map/ppermute | solution.py:249
  20.7 5.3 %collective-permute-start.7 = (bf16[16,2688]{1,0:T(8,128)(2,1)S(1)}, bf16[16,2688]{1,0:T(8,128)(2,1)S(1)}, u32[]{:S(2)}, u32[]{:S(2)}) collective-permute-start(bf16[16,2688]{1,0:T(8,128)(2,1)S(1)} %get-tuple-element.32), channel_id=1, source_target_pairs={{0,2},{2,0},{4,6},{6,4},{8,10},{10,8},{12,14},{14,12},{1,3},{3,1},... | collective-permute-start | bytes 258056 | tf_op jit(solution)/shard_map/ppermute | solution.py:249
  26.1 5.1 %collective-permute-start.8 = (bf16[8,2688]{1,0:T(8,128)(2,1)S(1)}, bf16[8,2688]{1,0:T(8,128)(2,1)S(1)}, u32[]{:S(2)}, u32[]{:S(2)}) collective-permute-start(bf16[8,2688]{1,0:T(8,128)(2,1)S(1)} %slice.12), channel_id=1, source_target_pairs={{0,8},{2,10},{4,12},{6,14},{8,0},{10,2},{12,4},{14,6},{1,9},{3,11}... | collective-permute-start | bytes 129032 | tf_op jit(solution)/shard_map/ppermute | solution.py:249

commit v4 on v3

--- a/solution.py
+++ b/solution.py
@@ -95,38 +95,34 @@
 
 def load_kernel(*refs):
     count = (len(refs) - 2) // 2
-    mark_ref, sems = refs[-2:]
+    sources, targets, sems = refs[1 : count + 1], refs[count + 1 : -1], refs[-1]
     copies = []
-    for i in range(count):
-        rows = refs[i].shape[0] // LOADS
+    for i, (source, target) in enumerate(zip(sources, targets)):
+        rows = source.shape[0] // LOADS
         for j in range(LOADS):
             part = pl.ds(j * rows, rows)
             copies.append(
-                pltpu.make_async_copy(
-                    refs[i].at[part], refs[count + i].at[part], sems.at[i * LOADS + j]
-                )
+                pltpu.make_async_copy(source.at[part], target.at[part], sems.at[i * LOADS + j])
             )
     for copy in copies:
         copy.start()
-    mark_ref[...] = jnp.zeros_like(mark_ref)
     for copy in copies:
         copy.wait()
 
 
-def pair_kernel(own_ref, came_ref, mark_ref, out_ref):
-    del mark_ref
+def pair_kernel(own_ref, came_ref, out_ref):
     both = jnp.concatenate([own_ref[...].astype(F32), came_ref[...].astype(F32)], axis=0)
     out_ref[...] = both.astype(BF16)
 
 
-def load(*arrays):
+def load(after, *arrays):
     return call(
         load_kernel,
-        [jax.ShapeDtypeStruct(a.shape, a.dtype) for a in arrays]
-        + [jax.ShapeDtypeStruct((8, 128), F32)],
+        [jax.ShapeDtypeStruct(a.shape, a.dtype) for a in arrays],
+        after,
         *arrays,
         scratch=[pltpu.SemaphoreType.DMA((LOADS * len(arrays),))],
-        here=range(len(arrays)),
+        here=range(1, len(arrays) + 1),
         cost=sum(2 * a.size * a.dtype.itemsize for a in arrays),
         room=50 * MIB,
     )
@@ -156,11 +152,13 @@
             out_ref[k, s * rows : (s + 1) * rows, :] = both.T
 
 
-def gate_up_kernel(own_ref, one_ref, two_ref, three_ref, gate_ref, up_ref, out_ref):
+def gate_up_kernel(own_ref, far_ref, *refs):
+    quad_refs, (gate_ref, up_ref, out_ref) = refs[:-3], refs[-3:]
     packed = own_ref.shape[1]
     piece = packed // PIECES
     hidden = gate_ref.shape[1]
-    x = jnp.concatenate([r[...] for r in (own_ref, one_ref, two_ref, three_ref)], axis=0)
+    pair = jnp.concatenate([own_ref[...].astype(F32), far_ref[...].astype(F32)], axis=0)
+    x = jnp.concatenate([pair.astype(BF16)] + [r[...] for r in quad_refs], axis=0)
     rows = x.shape[0]
     tall = jnp.concatenate([x[:, t * piece : (t + 1) * piece] for t in range(PIECES)], axis=0)
     place = lax.broadcasted_iota(jnp.int32, (rows, hidden), 0) % PACK
@@ -199,6 +197,15 @@
         part = (dot(main, down_ref[:, cols]) + last[t * rows : (t + 1) * rows]).astype(BF16)
         for b, ref in enumerate(out_refs):
             ref[:, cols] = part[b * count : (b + 1) * count]
+
+
+def sum_kernel(first_ref, *refs):
+    other_refs, (kept_ref, away_ref) = refs[:-2], refs[-2:]
+    total = first_ref[...].astype(F32)
+    for ref in other_refs:
+        total = total + ref[...].astype(F32)
+    kept_ref[...] = total[: kept_ref.shape[0]]
+    away_ref[...] = total[kept_ref.shape[0] :].astype(BF16)
 
 
 def mix_kernel(flight, kept_ref, came_ref, plan_ref, out_ref, held, sems):
@@ -248,6 +255,16 @@
     def swap(x, mask):
         return lax.ppermute(x, "expert", [(i, i ^ mask) for i in range(devices)])
 
+    def cross(x, mask):
+        perm = [(2 * i + c, 2 * (i ^ mask) + 1 - c) for i in range(devices) for c in range(2)]
+        return lax.ppermute(x, ("expert", "attn"), perm)
+
+    def flip(x):
+        return lax.ppermute(x, "attn", [(0, 1), (1, 0)])
+
+    def joined(x, y):
+        return call(pair_kernel, shape((2 * x.shape[0], packed), BF16), x, y)
+
     def across(x):
         if flight == 1:
             return x
@@ -269,7 +286,6 @@
         room=55169 * 1024,
     )
     sent = across(jnp.concatenate(sent, axis=1))
-    gate_proj, up_proj, mark = load(gate_proj, up_proj)
     plan = call(
         functools.partial(plan_kernel, flight),
         shape((flight, rows, 128), F32),
@@ -284,36 +300,38 @@
     )
     high = [bit for bit in (group >> n for n in range(1, group.bit_length())) if bit >= 4]
     block = sent
-    for bit in high:
-        block = call(
-            pair_kernel,
-            shape((2 * block.shape[0], packed), BF16),
-            block,
-            swap(block, bit),
-            mark,
-        )
-    came = [swap(block, mask) for mask in QUAD]
+    for bit in high[:-1]:
+        block = joined(block, swap(block, bit))
+    far = cross(block, high[-1])
+    pair = joined(flip(block), far)
+    came = [cross(pair, mask) for mask in QUAD]
+    gate_proj, up_proj = load(pair, gate_proj, up_proj)
     products = call(
         gate_up_kernel,
         shape((group * count, 2 * hidden_dev), F32),
         block,
+        flip(far),
         *came,
         gate_proj,
         up_proj,
     )
-    other = lax.ppermute(products, "attn", [(0, 1), (1, 0)])
-    parts = call(down_kernel, [shape(block.shape, BF16)] * 4, products, other, down_proj)
-    back = [swap(part, mask) for part, mask in zip(parts[1:], QUAD)]
-    summed = parts[0].astype(F32)
-    for x in back:
-        summed = summed + x.astype(F32)
-    for bit in reversed(high):
-        half_rows = summed.shape[0] // 2
-        kept, away = summed[:half_rows], summed[half_rows:].astype(BF16)
+    parts = call(down_kernel, [shape(pair.shape, BF16)] * 4, products, flip(products), down_proj)
+    back = [cross(part, mask) for part, mask in zip(parts[1:], QUAD)]
+    kept, away = call(
+        sum_kernel,
+        [shape(block.shape, F32), shape(block.shape, BF16)],
+        *back[1:],
+        flip(parts[0]),
+        back[0],
+    )
+    kept, came_back = flip(kept), cross(away, high[-1])
+    for bit in reversed(high[:-1]):
+        summed = kept + came_back.astype(F32)
+        rows_in = summed.shape[0] // 2
+        kept, away = summed[:rows_in], summed[rows_in:].astype(BF16)
         came_back = swap(away, bit)
-        summed = kept + came_back.astype(F32)
     if flight > 1:
-        kept = across(summed.astype(BF16)).astype(F32)
+        kept = across((kept + came_back.astype(F32)).astype(BF16)).astype(F32)
         came_back = jnp.zeros(kept.shape, BF16)
     mixed = call(
         functools.partial(mix_kernel, flight),

time: 32.4 us -> 32 us (0.988)
  waiting for transfers between devices: 12.2 us -> 10.1 us
  starting transfers between devices: 13.6 us -> 15.2 us
    ppermute x9 -> x13, waiting for transfers between devices: 12.2 us -> 10.1 us  [the longest x8 8.86 us: cross(): return lax.ppermute(x, ('expert', 'attn'), perm)]
    ppermute x9 -> x13, starting transfers between devices: 13.6 us -> 15.2 us  [the longest x8 13.8 us: cross(): return lax.ppermute(x, ('expert', 'attn'), perm)]
    pallas_call x7 -> x8, Pallas kernels: 6.17 us -> 6.24 us  [call(): pl.pallas_call(kernel, out_shape=out_shape, in_specs=[hbm if i in here el...]
  transfers between devices with their start and end apart: 9 -> 13, of which waited for: 9 -> 7; matrix products, arithmetic and copies ran while one was open for 0% -> 0% of each run, Pallas kernels for 7% -> 7%
where the time goes in v4:
time: 32 us; the launch traced here: 31.8 us
  starting transfers between devices  15.2 us (48%)
  waiting for transfers between devices  10.1 us (32%)
  Pallas kernels  6.24 us (20%)
    ppermute x8, starting transfers between devices, cross(): return lax.ppermute(x, ('expert', 'attn'), perm)  13.8 us
    ppermute x8, waiting for transfers between devices, cross(): return lax.ppermute(x, ('expert', 'attn'), perm)  8.86 us
    pallas_call x8, Pallas kernels, call(): pl.pallas_call(kernel, out_shape=out_shape, in_specs=[hbm if i in here el...  6.24 us
    ppermute x5, starting transfers between devices, flip(): return lax.ppermute(x, 'attn', [(0, 1), (1, 0)])  1.37 us
    ppermute x5, waiting for transfers between devices, flip(): return lax.ppermute(x, 'attn', [(0, 1), (1, 0)])  1.24 us
  transfers between devices with their start and end apart: 13, of which 7 were waited for; matrix products, arithmetic and copies ran while one was open for 0% of the time, Pallas kernels for 7%

profile of v4, /device:TPU:0, one launch (start us, length us, event | category | flops | bytes accessed | tf_op | source)
XLA Modules:
  0.0 31.8 jit_solution(1951733411072970165)
XLA Ops:
  0.0 1.5 %shard_map.64 = (bf16[8,384]{1,0:T(8,128)(2,1)S(1)}, bf16[8,384]{1,0:T(8,128)(2,1)S(1)}, bf16[8,384]{1,0:T(8,128)(2,1)S(1)}, bf16[8,384]{1,0:T(8,128)(2,1)S(1)},...) custom-call(bf16[3,32,3584]{2,1,0:T(8,128)(2,1)} %tokens_ref.1, ...), custom_call_target="tpu_custom_call" | custom-call | tf_op jit(solution)/shard_map/pallas_call | solution.py:27
  1.6 3.5 %collective-permute-start = (bf16[8,2688]{1,0:T(8,128)(2,1)S(1)}, bf16[8,2688]{1,0:T(8,128)(2,1)S(1)}, u32[]{:S(2)}, u32[]{:S(2)}) collective-permute-start(bf16[8,2688]{1,0:T(8,128)(2,1)S(1)} %constant_dynamic-update-slice_fusion.own_ref), channel_id=1, source_target_pairs={{0,9},{1,8},{2,11},{3,10},{4,13},{5,12},{6,15},{7,14},{8,1},{9,0},... | collective-permute-start | bytes 129032 | tf_op jit(solution)/shard_map/ppermute | solution.py:260
  5.1 0.7 %collective-permute-start.2 = (bf16[8,2688]{1,0:T(8,128)(2,1)S(1)}, bf16[8,2688]{1,0:T(8,128)(2,1)S(1)}, u32[]{:S(2)}, u32[]{:S(2)}) collective-permute-start(bf16[8,2688]{1,0:T(8,128)(2,1)S(1)} %constant_dynamic-update-slice_fusion.own_ref), channel_id=1, source_target_pairs={{0,1},{1,0},{2,3},{3,2},{4,5},{5,4},{6,7},{7,6},{8,9},{9,8},{10,11... | collective-permute-start | bytes 129032 | tf_op jit(solution)/shard_map/ppermute | solution.py:263
  5.8 1.3 %collective-permute-done.came_ref = bf16[8,2688]{1,0:T(8,128)(2,1)S(1)} collective-permute-done((bf16[8,2688]{1,0:T(8,128)(2,1)S(1)}, bf16[8,2688]{1,0:T(8,128)(2,1)S(1)}, u32[]{:S(2)}, u32[]{:S(2)}) %collective-permute-start) | collective-permute-done | bytes 43040 | tf_op jit(solution)/shard_map/ppermute | solution.py:260
  7.1 0.0 collective-permute-done.2.own_ref
  7.1 3.1 %collective-permute-start.3 = (bf16[16,2688]{1,0:T(8,128)(2,1)S(1)}, bf16[16,2688]{1,0:T(8,128)(2,1)S(1)}, u32[]{:S(2)}, u32[]{:S(2)}) collective-permute-start(bf16[16,2688]{1,0:T(8,128)(2,1)S(1)} %shard_map.65.refs_0_), channel_id=1, source_target_pairs={{0,7},{1,6},{2,5},{3,4},{4,3},{5,2},{6,1},{7,0},{8,15},{9,14},{10,... | collective-permute-start | bytes 258056 | tf_op jit(solution)/shard_map/ppermute | solution.py:260
  10.2 0.2 collective-permute-start.4
  10.4 0.4 %collective-permute-start.5 = (bf16[16,2688]{1,0:T(8,128)(2,1)S(1)}, bf16[16,2688]{1,0:T(8,128)(2,1)S(1)}, u32[]{:S(2)}, u32[]{:S(2)}) collective-permute-start(bf16[16,2688]{1,0:T(8,128)(2,1)S(1)} %shard_map.65.refs_0_), channel_id=1, source_target_pairs={{0,3},{1,2},{2,1},{3,0},{4,7},{5,6},{6,5},{7,4},{8,11},{9,10},{10,... | collective-permute-start | bytes 258056 | tf_op jit(solution)/shard_map/ppermute | solution.py:260
  10.9 0.1 collective-permute-start.1
  11.0 2.1 %shard_map.66 = (bf16[3584,256]{1,0:T(8,128)(2,1)S(1)}, bf16[3584,256]{1,0:T(8,128)(2,1)S(1)}) custom-call(bf16[16,2688]{1,0:T(8,128)(2,1)S(1)} %shard_map.65.refs_0_, bf16[3584,256]{1,0:T(8,128)(2,1)} %refs_1_.1, bf16[3584,256]{1,0:T(8,128)(2,1)} %refs_2_.1), custom_call_target="tpu_custom_call" | custom-call | bytes 7340032 | tf_op jit(solution)/shard_map/pallas_call | solution.py:27
  13.1 0.0 collective-permute-done.1.far_ref
  13.1 0.1 collective-permute-done.3.refs_0_
  13.1 1.9 %collective-permute-done.4.refs_1_ = bf16[16,2688]{1,0:T(8,128)(2,1)S(1)} collective-permute-done((bf16[16,2688]{1,0:T(8,128)(2,1)S(1)}, bf16[16,2688]{1,0:T(8,128)(2,1)S(1)}, u32[]{:S(2)}, u32[]{:S(2)}) %collective-permute-start.4) | collective-permute-done | bytes 86048 | tf_op jit(solution)/shard_map/ppermute | solution.py:260
  15.1 0.0 collective-permute-done.5.refs_2_
  15.1 0.0 copy-start
  15.1 0.8 %shard_map.67.mine_ref = f32[64,512]{1,0:T(8,128)S(1)} custom-call(bf16[8,2688]{1,0:T(8,128)(2,1)S(1)} %constant_dynamic-update-slice_fusion.own_ref, bf16[8,2688]{1,0:T(8,128)(2,1)S(1)} %collective-permute-done.1.far_ref, bf16[16,2688]{1,0:T(8,128)(2,1)S(1)} %collective-permute-done.3.refs_0_, bf16[16,2688]{1,0:T(8,128)(2,1)S(1)} %collective-permute-done.4.refs_1_, ...), custom_call_target="tpu_custom_call" | custom-call | tf_op jit(solution)/shard_map/pallas_call | solution.py:27
  15.9 0.0 copy-start.1
  15.9 0.0 copy-start.2
  15.9 0.2 collective-permute-start.6
  16.1 1.2 %collective-permute-done.6.peer_ref = f32[64,512]{1,0:T(8,128)S(1)} collective-permute-done((f32[64,512]{1,0:T(8,128)S(1)}, f32[64,512]{1,0:T(8,128)S(1)}, u32[]{:S(2)}, u32[]{:S(2)}) %collective-permute-start.6) | collective-permute-done | bytes 131104 | tf_op jit(solution)/shard_map/ppermute | solution.py:263
  17.3 0.0 copy-done
  17.3 0.5 %shard_map.68 = (bf16[16,2688]{1,0:T(8,128)(2,1)S(1)}, bf16[16,2688]{1,0:T(8,128)(2,1)S(1)}, bf16[16,2688]{1,0:T(8,128)(2,1)S(1)}, bf16[16,2688]{1,0:T(8,128)(2,1)S(1)}) custom-call(f32[64,512]{1,0:T(8,128)S(1)} %shard_map.67.mine_ref, f32[64,512]{1,0:T(8,128)S(1)} %collective-permute-done.6.peer_ref, bf16[256,3584]{1,0:T(8,128)(2,1)S(1)} %copy-done), custom_call_target="tpu_custom_call" | custom-call | tf_op jit(solution)/shard_map/pallas_call | solution.py:27
  17.8 2.8 %collective-permute-start.10 = (bf16[16,2688]{1,0:T(8,128)(2,1)S(1)}, bf16[16,2688]{1,0:T(8,128)(2,1)S(1)}, u32[]{:S(2)}, u32[]{:S(2)}) collective-permute-start(bf16[16,2688]{1,0:T(8,128)(2,1)S(1)} %get-tuple-element.32), channel_id=1, source_target_pairs={{0,7},{1,6},{2,5},{3,4},{4,3},{5,2},{6,1},{7,0},{8,15},{9,14},{10,... | collective-permute-start | bytes 258056 | tf_op jit(solution)/shard_map/ppermute | solution.py:260
  20.6 0.1 collective-permute-start.7
  20.8 0.5 %collective-permute-start.8 = (bf16[16,2688]{1,0:T(8,128)(2,1)S(1)}, bf16[16,2688]{1,0:T(8,128)(2,1)S(1)}, u32[]{:S(2)}, u32[]{:S(2)}) collective-permute-start(bf16[16,2688]{1,0:T(8,128)(2,1)S(1)} %get-tuple-element.30), channel_id=1, source_target_pairs={{0,3},{1,2},{2,1},{3,0},{4,7},{5,6},{6,5},{7,4},{8,11},{9,10},{10,... | collective-permute-start | bytes 258056 | tf_op jit(solution)/shard_map/ppermute | solution.py:260
  21.2 0.2 collective-permute-start.9
  21.4 2.1 %collective-permute-done.10.refs_2_ = bf16[16,2688]{1,0:T(8,128)(2,1)S(1)} collective-permute-done((bf16[16,2688]{1,0:T(8,128)(2,1)S(1)}, bf16[16,2688]{1,0:T(8,128)(2,1)S(1)}, u32[]{:S(2)}, u32[]{:S(2)}) %collective-permute-start.10) | collective-permute-done | bytes 86048 | tf_op jit(solution)/shard_map/ppermute | solution.py:260
  23.5 1.8 %collective-permute-done.7.first_ref = bf16[16,2688]{1,0:T(8,128)(2,1)S(1)} collective-permute-done((bf16[16,2688]{1,0:T(8,128)(2,1)S(1)}, bf16[16,2688]{1,0:T(8,128)(2,1)S(1)}, u32[]{:S(2)}, u32[]{:S(2)}) %collective-permute-start.7) | collective-permute-done | bytes 86048 | tf_op jit(solution)/shard_map/ppermute | solution.py:260
  25.4 0.0 collective-permute-done.8.refs_0_
  25.4 0.0 collective-permute-done.9.refs_1_
  25.4 0.2 collective-permute-start.11
  25.6 3.2 %collective-permute-start.12 = (bf16[8,2688]{1,0:T(8,128)(2,1)S(1)}, bf16[8,2688]{1,0:T(8,128)(2,1)S(1)}, u32[]{:S(2)}, u32[]{:S(2)}) collective-permute-start(bf16[8,2688]{1,0:T(8,128)(2,1)S(1)} %get-tuple-element.34), channel_id=1, source_target_pairs={{0,9},{1,8},{2,11},{3,10},{4,13},{5,12},{6,15},{7,14},{8,1},{9,0},... | collective-permute-start | bytes 129032 | tf_op jit(solution)/shard_map/ppermute | solution.py:260
  28.8 0.0 copy-done.1
  28.8 0.0 copy-done.2
  28.8 0.3 shard_map.70.plan_ref
  29.1 1.6 %collective-permute-done.12.came_ref = bf16[8,2688]{1,0:T(8,128)(2,1)S(1)} collective-permute-done((bf16[8,2688]{1,0:T(8,128)(2,1)S(1)}, bf16[8,2688]{1,0:T(8,128)(2,1)S(1)}, u32[]{:S(2)}, u32[]{:S(2)}) %collective-permute-start.12) | collective-permute-done | bytes 43040 | tf_op jit(solution)/shard_map/ppermute | solution.py:260
  30.7 0.0 collective-permute-done.11.kept_ref
  30.7 1.1 %shard_map.71 = bf16[96,3584]{1,0:T(8,128)(2,1)} custom-call(f32[8,2688]{1,0:T(8,128)S(1)} %collective-permute-done.11.kept_ref, bf16[8,2688]{1,0:T(8,128)(2,1)S(1)} %collective-permute-done.12.came_ref, f32[1,96,128]{2,1,0:T(8,128)S(1)} %shard_map.70.plan_ref), custom_call_target="tpu_custom_call" | custom-call | tf_op jit(solution)/shard_map/pallas_call | solution.py:27
  (9 shorter events, 0.1 us)
Async XLA Ops:
  1.6 5.5 %collective-permute-start = (bf16[8,2688]{1,0:T(8,128)(2,1)S(1)}, bf16[8,2688]{1,0:T(8,128)(2,1)S(1)}, u32[]{:S(2)}, u32[]{:S(2)}) collective-permute-start(bf16[8,2688]{1,0:T(8,128)(2,1)S(1)} %constant_dynamic-update-slice_fusion.own_ref), channel_id=1, source_target_pairs={{0,9},{1,8},{2,11},{3,10},{4,13},{5,12},{6,15},{7,14},{8,1},{9,0},... | collective-permute-start | bytes 129032 | tf_op jit(solution)/shard_map/ppermute | solution.py:260
  5.1 2.0 %collective-permute-start.2 = (bf16[8,2688]{1,0:T(8,128)(2,1)S(1)}, bf16[8,2688]{1,0:T(8,128)(2,1)S(1)}, u32[]{:S(2)}, u32[]{:S(2)}) collective-permute-start(bf16[8,2688]{1,0:T(8,128)(2,1)S(1)} %constant_dynamic-update-slice_fusion.own_ref), channel_id=1, source_target_pairs={{0,1},{1,0},{2,3},{3,2},{4,5},{5,4},{6,7},{7,6},{8,9},{9,8},{10,11... | collective-permute-start | bytes 129032 | tf_op jit(solution)/shard_map/ppermute | solution.py:263
  7.1 6.0 %collective-permute-start.3 = (bf16[16,2688]{1,0:T(8,128)(2,1)S(1)}, bf16[16,2688]{1,0:T(8,128)(2,1)S(1)}, u32[]{:S(2)}, u32[]{:S(2)}) collective-permute-start(bf16[16,2688]{1,0:T(8,128)(2,1)S(1)} %shard_map.65.refs_0_), channel_id=1, source_target_pairs={{0,7},{1,6},{2,5},{3,4},{4,3},{5,2},{6,1},{7,0},{8,15},{9,14},{10,... | collective-permute-start | bytes 258056 | tf_op jit(solution)/shard_map/ppermute | solution.py:260
  10.2 4.8 %collective-permute-start.4 = (bf16[16,2688]{1,0:T(8,128)(2,1)S(1)}, bf16[16,2688]{1,0:T(8,128)(2,1)S(1)}, u32[]{:S(2)}, u32[]{:S(2)}) collective-permute-start(bf16[16,2688]{1,0:T(8,128)(2,1)S(1)} %shard_map.65.refs_0_), channel_id=1, source_target_pairs={{0,5},{1,4},{2,7},{3,6},{4,1},{5,0},{6,3},{7,2},{8,13},{9,12},{10,... | collective-permute-start | bytes 258056 | tf_op jit(solution)/shard_map/ppermute | solution.py:260
  10.4 4.6 %collective-permute-start.5 = (bf16[16,2688]{1,0:T(8,128)(2,1)S(1)}, bf16[16,2688]{1,0:T(8,128)(2,1)S(1)}, u32[]{:S(2)}, u32[]{:S(2)}) collective-permute-start(bf16[16,2688]{1,0:T(8,128)(2,1)S(1)} %shard_map.65.refs_0_), channel_id=1, source_target_pairs={{0,3},{1,2},{2,1},{3,0},{4,7},{5,6},{6,5},{7,4},{8,11},{9,10},{10,... | collective-permute-start | bytes 258056 | tf_op jit(solution)/shard_map/ppermute | solution.py:260
  10.9 2.2 %collective-permute-start.1 = (bf16[8,2688]{1,0:T(8,128)(2,1)S(1)}, bf16[8,2688]{1,0:T(8,128)(2,1)S(1)}, u32[]{:S(2)}, u32[]{:S(2)}) collective-permute-start(bf16[8,2688]{1,0:T(8,128)(2,1)S(1)} %collective-permute-done.came_ref), channel_id=1, source_target_pairs={{0,1},{1,0},{2,3},{3,2},{4,5},{5,4},{6,7},{7,6},{8,9},{9,8},{10,11... | collective-permute-start | bytes 129032 | tf_op jit(solution)/shard_map/ppermute | solution.py:263
  15.1 2.3 %copy-start = (bf16[256,3584]{1,0:T(8,128)(2,1)S(1)}, bf16[256,3584]{1,0:T(8,128)(2,1)}, u32[]{:S(2)}) copy-start(bf16[256,3584]{1,0:T(8,128)(2,1)} %down_ref.1) | copy-start | bytes 5505028
  15.9 12.9 %copy-start.1 = (s32[3,32,8]{1,2,0:T(8,128)S(1)}, s32[3,32,8]{1,2,0:T(8,128)}, u32[]{:S(2)}) copy-start(s32[3,32,8]{1,2,0:T(8,128)} %param.7) | copy-start | bytes 9220
  15.9 12.9 %copy-start.2 = (f32[3,32,8]{1,2,0:T(8,128)S(1)}, f32[3,32,8]{1,2,0:T(8,128)}, u32[]{:S(2)}) copy-start(f32[3,32,8]{1,2,0:T(8,128)} %param.8) | copy-start | bytes 9220
  15.9 1.4 %collective-permute-start.6 = (f32[64,512]{1,0:T(8,128)S(1)}, f32[64,512]{1,0:T(8,128)S(1)}, u32[]{:S(2)}, u32[]{:S(2)}) collective-permute-start(f32[64,512]{1,0:T(8,128)S(1)} %shard_map.67.mine_ref), channel_id=1, source_target_pairs={{0,1},{1,0},{2,3},{3,2},{4,5},{5,4},{6,7},{7,6},{8,9},{9,8},{10,11... | collective-permute-start | bytes 393224 | tf_op jit(solution)/shard_map/ppermute | solution.py:263
  17.8 5.7 %collective-permute-start.10 = (bf16[16,2688]{1,0:T(8,128)(2,1)S(1)}, bf16[16,2688]{1,0:T(8,128)(2,1)S(1)}, u32[]{:S(2)}, u32[]{:S(2)}) collective-permute-start(bf16[16,2688]{1,0:T(8,128)(2,1)S(1)} %get-tuple-element.32), channel_id=1, source_target_pairs={{0,7},{1,6},{2,5},{3,4},{4,3},{5,2},{6,1},{7,0},{8,15},{9,14},{10,... | collective-permute-start | bytes 258056 | tf_op jit(solution)/shard_map/ppermute | solution.py:260
  20.6 4.8 %collective-permute-start.7 = (bf16[16,2688]{1,0:T(8,128)(2,1)S(1)}, bf16[16,2688]{1,0:T(8,128)(2,1)S(1)}, u32[]{:S(2)}, u32[]{:S(2)}) collective-permute-start(bf16[16,2688]{1,0:T(8,128)(2,1)S(1)} %get-tuple-element.29), channel_id=1, source_target_pairs={{0,5},{1,4},{2,7},{3,6},{4,1},{5,0},{6,3},{7,2},{8,13},{9,12},{10,... | collective-permute-start | bytes 258056 | tf_op jit(solution)/shard_map/ppermute | solution.py:260
  20.8 4.6 %collective-permute-start.8 = (bf16[16,2688]{1,0:T(8,128)(2,1)S(1)}, bf16[16,2688]{1,0:T(8,128)(2,1)S(1)}, u32[]{:S(2)}, u32[]{:S(2)}) collective-permute-start(bf16[16,2688]{1,0:T(8,128)(2,1)S(1)} %get-tuple-element.30), channel_id=1, source_target_pairs={{0,3},{1,2},{2,1},{3,0},{4,7},{5,6},{6,5},{7,4},{8,11},{9,10},{10,... | collective-permute-start | bytes 258056 | tf_op jit(solution)/shard_map/ppermute | solution.py:260
  21.2 4.2 %collective-permute-start.9 = (bf16[16,2688]{1,0:T(8,128)(2,1)S(1)}, bf16[16,2688]{1,0:T(8,128)(2,1)S(1)}, u32[]{:S(2)}, u32[]{:S(2)}) collective-permute-start(bf16[16,2688]{1,0:T(8,128)(2,1)S(1)} %get-tuple-element.31), channel_id=1, source_target_pairs={{0,1},{1,0},{2,3},{3,2},{4,5},{5,4},{6,7},{7,6},{8,9},{9,8},{10,11... | collective-permute-start | bytes 258056 | tf_op jit(solution)/shard_map/ppermute | solution.py:263
  25.4 5.2 %collective-permute-start.11 = (f32[8,2688]{1,0:T(8,128)S(1)}, f32[8,2688]{1,0:T(8,128)S(1)}, u32[]{:S(2)}, u32[]{:S(2)}) collective-permute-start(f32[8,2688]{1,0:T(8,128)S(1)} %get-tuple-element.33), channel_id=1, source_target_pairs={{0,1},{1,0},{2,3},{3,2},{4,5},{5,4},{6,7},{7,6},{8,9},{9,8},{10,11... | collective-permute-start | bytes 258056 | tf_op jit(solution)/shard_map/ppermute | solution.py:263
  25.6 5.0 %collective-permute-start.12 = (bf16[8,2688]{1,0:T(8,128)(2,1)S(1)}, bf16[8,2688]{1,0:T(8,128)(2,1)S(1)}, u32[]{:S(2)}, u32[]{:S(2)}) collective-permute-start(bf16[8,2688]{1,0:T(8,128)(2,1)S(1)} %get-tuple-element.34), channel_id=1, source_target_pairs={{0,9},{1,8},{2,11},{3,10},{4,13},{5,12},{6,15},{7,14},{8,1},{9,0},... | collective-permute-start | bytes 129032 | tf_op jit(solution)/shard_map/ppermute | solution.py:260
